TPU v7x, 32 devices: a whole 2x2x4 slice. The times are simulated.
32 devices in a mesh: days: 2 (over x), blk: 16 (over z, y, core).
Axes of the slice: x: 2, y: 2, z: 4, core: 2. Of those that a mesh axis runs over, the one named last changes fastest.
Arguments:
- traces: bfloat16 [2048, 8, 1024], P(('days', 'blk')), parts along dimension 0, may hold values from -6 to 6
- valid: int32 [32, 8], P(('days', 'blk')), parts along dimension 0, may hold values from 0 to 1, as said below
Outputs:
- correlations: bfloat16 [2, 32, 64, 64, 512], P(None, ('days', 'blk')), parts along dimension 1
There are 2 independent parts, one for each index of `days`. A program takes and returns all parts, laid end to end along the dimension named above; each array names one. Nothing has to cross between parts.
Inputs may be any that keep to these rules, and one draw needn't show every extreme that they name: `valid`: in every draw one block, which one is drawn from the seed, has no usable window at all.
All inputs are finite; a program needn't handle non-finite values.
Results may differ from a plain program's by a relative error of at most 0.0089.
Values may be sent and summed in bfloat16 or wider, within the bound.
No kernel may reach another device: no remote copies, remote signals or barrier semaphores. Data moves between devices by JAX's collectives and lax.ppermute only.
A program may use at most 128 MiB of HBM per device.

v0:
```python
import math

import jax
import jax.numpy as jnp
from jax import lax
from jax.sharding import PartitionSpec as P

CH = 64
WINDOW_SAMPLES = 1024
LAGS = 512
BAND = 64
ROUNDS = 2
TIME_WINDOWS = 8
FREQS = 512


epsilon = 1e-05


def passed_along(block, axis, distance):
    devices = range(lax.axis_size(axis))
    route = [(i - distance, i) for i in devices if i - distance in devices]
    return lax.ppermute(block, axis, route)


def from_behind(block, axis, distance):
    devices = range(lax.axis_size(axis))
    route = [((i - distance) % len(devices), i) for i in devices]
    return lax.ppermute(block, axis, route)


def forward_twiddles():
    samples = jnp.arange(WINDOW_SAMPLES, dtype=jnp.int32)
    bins = jnp.arange(FREQS, dtype=jnp.int32)
    phase = (samples[:, None] * bins[None, :] % WINDOW_SAMPLES).astype(jnp.float32) * (
        2.0 * math.pi / WINDOW_SAMPLES
    )
    table = jnp.concatenate([jnp.cos(phase), -jnp.sin(phase)], axis=1) / math.sqrt(WINDOW_SAMPLES)
    return table.astype(jnp.bfloat16)


def inverse_table():
    bins = jnp.arange(FREQS, dtype=jnp.int32)
    shifts = jnp.arange(LAGS, dtype=jnp.int32) - LAGS // 2
    phase = (bins[:, None] * shifts[None, :] % WINDOW_SAMPLES).astype(jnp.float32) * (
        2.0 * math.pi / WINDOW_SAMPLES
    )
    weight = jnp.where(bins == 0, 1.0, 2.0).astype(jnp.float32)[:, None] / math.sqrt(FREQS)
    table = jnp.concatenate([weight * jnp.cos(phase), -weight * jnp.sin(phase)], axis=0)
    return table.astype(jnp.bfloat16)


def whiten(traces, prior_sample, flags):
    pair_count = traces.shape[0]
    differenced_traces = (traces.astype(jnp.float32) - prior_sample.astype(jnp.float32)).astype(
        jnp.bfloat16
    )
    window_spectra = jnp.dot(
        differenced_traces.reshape(pair_count * TIME_WINDOWS, WINDOW_SAMPLES),
        forward_twiddles(),
        preferred_element_type=jnp.float32,
    )
    window_spectra = window_spectra.reshape(pair_count, TIME_WINDOWS, 2 * FREQS)
    power = window_spectra[:, :, :FREQS] ** 2 + window_spectra[:, :, FREQS:] ** 2
    banded = jnp.mean(power.reshape(pair_count, TIME_WINDOWS, FREQS // BAND, BAND), axis=-1)
    factor = jnp.repeat(lax.rsqrt(banded + epsilon), BAND, axis=-1) * flags[:, :, None]
    return (window_spectra * jnp.concatenate([factor, factor], axis=-1)).astype(jnp.bfloat16)


def correlate(own, partner, own_flags, partner_flags, inverse_parts):
    own_real = own[:, :, :FREQS]
    own_imag = own[:, :, FREQS:]
    far_real = partner[:, :, :FREQS]
    far_imag = partner[:, :, FREQS:]
    left_side = jnp.concatenate([own_real, own_imag], axis=1)
    real_rows = jnp.concatenate([far_real, far_imag], axis=1)
    imag_rows = jnp.concatenate([far_imag, -far_real], axis=1)
    right_side = jnp.concatenate([real_rows, imag_rows], axis=0)
    cross = jnp.einsum("iuf,kuf->fik", left_side, right_side, preferred_element_type=jnp.float32)
    total = jnp.maximum(jnp.sum(own_flags * partner_flags), 1.0)
    stacked = (cross / total).astype(jnp.bfloat16).reshape(FREQS, CH, 2, CH)
    result = lax.dot_general(
        stacked, inverse_parts, (((0, 2), (1, 0)), ((), ())), preferred_element_type=jnp.float32
    )
    return result.astype(jnp.bfloat16)


def shards(traces, valid):
    last_row = traces[CH - 1 :]
    before = passed_along(last_row, "blk", 1)
    prior_sample = jnp.concatenate([before, traces[:-1]], axis=0)
    own_flags = valid.astype(jnp.float32)
    whitened = whiten(traces, prior_sample, jnp.broadcast_to(own_flags, (CH, TIME_WINDOWS)))
    flag_wire = valid.astype(jnp.bfloat16)
    inverse_parts = inverse_table().reshape(2, FREQS, LAGS)
    held = (whitened, flag_wire)
    results = []
    for round_index in range(1, ROUNDS + 1):
        held = from_behind((whitened, flag_wire), "blk", -round_index)
        results.append(
            correlate(
                whitened, held[0], own_flags[0], held[1][0].astype(jnp.float32), inverse_parts
            )
        )
    return jnp.stack(results, axis=0)[:, None]


def solution(mesh):
    return jax.shard_map(
        shards,
        mesh=mesh,
        in_specs=(P(("days", "blk"), None, None), P(("days", "blk"), None)),
        out_specs=P(None, ("days", "blk"), None, None, None),
        check_vma=False,
    )
```

profile of v0, /device:TPU:1, one launch (start us, length us, event | category | flops | bytes accessed | tf_op | source)
XLA Modules:
  0.0 117.8 jit_solution(2148790233332401265)
XLA Ops:
  0.0 0.7 convert_bitcast_fusion
  0.8 5.7 %collective-permute-start.4 = (bf16[1,8]{1,0:T(2,128)(2,1)S(1)}, bf16[1,8]{1,0:T(2,128)(2,1)S(1)}, u32[]{:S(2)}, u32[]{:S(2)}) collective-permute-start(bf16[1,8]{1,0:T(2,128)(2,1)S(1)} %get-tuple-element.18), channel_id=1, source_target_pairs={{2,0},{3,1},{4,2},{5,3},{6,4},{7,5},{8,6},{9,7},{10,8},{11,9},{12,... | collective-permute-start | bytes 56 | tf_op jit(solution)/shard_map/ppermute | solution.py:29
  6.5 0.7 slice.32
  7.2 3.4 %collective-permute-start = (bf16[1,8,1024]{2,1,0:T(8,128)(2,1)S(1)}, bf16[1,8,1024]{2,1,0:T(8,128)(2,1)S(1)}, u32[]{:S(2)}, u32[]{:S(2)}) collective-permute-start(bf16[1,8,1024]{2,1,0:T(8,128)(2,1)S(1)} %slice.32), channel_id=1, source_target_pairs={{0,1},{1,2},{2,3},{3,4},{4,5},{5,6},{6,7},{7,8},{8,9},{9,10},{10,1... | collective-permute-start | bytes 49160 | tf_op jit(solution)/shard_map/ppermute | solution.py:23
  10.6 8.2 %sine_negate_fusion = (f32[1024,512]{1,0:T(8,128)S(1)}, f32[1024,512]{1,0:T(8,128)S(1)}) fusion(), kind=kLoop, calls=%fused_computation.22 | loop fusion | flops 7864320 | bytes 4194304 | tf_op jit(solution)/shard_map/neg | solution.py:38
  18.9 1.3 %fusion.7 = f32[64,8,1024]{2,1,0:T(8,128)S(1)} fusion(f32[1024,512]{1,0:T(8,128)S(1)} %get-tuple-element.19, f32[1024,512]{1,0:T(8,128)S(1)} %get-tuple-element.20, bf16[64,8,1024]{2,1,0:T(8,128)(2,1)S(1)} %copy-done.4, bf16[63,8,1024]{2,1,0:T(8,128)(2,1)S(1)} %slice-done, bf16[1,8,1024]{2,1,0:T(8,128)(2,1)S(1)} %collective-permute-done), kind=kOutput, calls=%fused_computation.16 | convolution fusion | flops 1079508992 | bytes 8388608 | tf_op jit(solution)/shard_map/dot_general | solution.py:58
  20.2 1.3 %copy-done.1 = f32[64,8,1024]{2,1,0:T(8,128)} copy-done((f32[64,8,1024]{2,1,0:T(8,128)}, f32[64,8,1024]{2,1,0:T(8,128)S(1)}, u32[]{:S(2)}) %copy-start.1) | copy-done | bytes 2097176
  23.7 0.7 reshape.40
  24.6 1.4 %copy-done.2 = f32[64,8,1024]{2,1,0:T(8,128)S(1)} copy-done((f32[64,8,1024]{2,1,0:T(8,128)S(1)}, f32[64,8,1024]{2,1,0:T(8,128)}, u32[]{:S(2)}) %copy-start.2) | copy-done | bytes 2097176
  26.6 4.4 %multiply_convert_fusion.1 = (bf16[512,512]{1,0:T(8,128)(2,1)S(1)}, bf16[512,512]{1,0:T(8,128)(2,1)S(1)}) fusion(s32[512]{0:T(512)S(1)} %iota_add_fusion, f32[512]{0:T(512)S(1)} %get-tuple-element.21, f32[512]{0:T(512)S(1)} %get-tuple-element.22), kind=kLoop, calls=%fused_computation.42 | loop fusion | flops 4718592 | bytes 1054720 | tf_op jit(solution)/shard_map/convert.2
  31.0 1.0 pad_maximum_fusion.1
  32.0 0.6 fusion.27
  34.3 3.5 %copy.27 = bf16[64,16,512]{0,1,2:T(8,128)(2,1)} copy(bf16[64,16,512]{2,1,0:T(8,128)(2,1)S(1)} %pad_maximum_fusion) | data formatting | bytes 2097152 | tf_op jit(solution)/shard_map/concatenate | solution.py:75
  37.7 7.2 %collective-permute-done.1 = bf16[64,8,1024]{2,1,0:T(8,128)(2,1)S(1)} collective-permute-done((bf16[64,8,1024]{2,1,0:T(8,128)(2,1)S(1)}, bf16[64,8,1024]{2,1,0:T(8,128)(2,1)S(1)}, u32[]{:S(2)}, u32[]{:S(2)}) %collective-permute-start.1) | collective-permute-done | bytes 1048608 | tf_op jit(solution)/shard_map/ppermute | solution.py:29
  45.3 3.9 %copy.28 = bf16[128,16,512]{0,1,2:T(8,128)(2,1)} copy(bf16[128,16,512]{2,1,0:T(8,128)(2,1)S(1)} %maximum_maximum_fusion) | data formatting | bytes 4194304 | tf_op jit(solution)/shard_map/concatenate | solution.py:78
  49.2 8.2 %divide_convert_fusion.1 = bf16[512,64,128]{2,1,0:T(8,128)(2,1)} fusion(f32[]{:T(128)S(6)} %max.6, bf16[64,16,512]{0,1,2:T(8,128)(2,1)} %copy.27, bf16[128,16,512]{0,1,2:T(8,128)(2,1)} %copy.28), kind=kOutput, calls=%fused_computation.1 | convolution fusion | flops 142606336 | bytes 11534340 | tf_op jit(solution)/shard_map/iuf,kuf->fik/dot_general | solution.py:79
  57.4 12.9 %copy.29 = bf16[512,64,128]{0,2,1:T(8,128)(2,1)} copy(bf16[512,64,128]{2,1,0:T(8,128)(2,1)} %divide_convert_fusion.1) | data formatting | bytes 16777216 | tf_op jit(solution)/shard_map/convert_element_type | solution.py:81
  70.3 1.3 %fusion.32 = (bf16[64,8,512]{2,1,0:T(8,128)(2,1)S(1)}, bf16[64,8,512]{2,1,0:T(8,128)(2,1)S(1)}, bf16[64,8,512]{2,1,0:T(8,128)(2,1)S(1)}) fusion(bf16[64,8,1024]{2,1,0:T(8,128)(2,1)} %collective-permute-done.3), kind=kLoop, calls=%fused_computation.64 | loop fusion | flops 262144 | bytes 2621440 | tf_op jit(solution)/shard_map/slice | solution.py:73
  71.9 3.9 %copy.31 = bf16[128,16,512]{0,1,2:T(8,128)(2,1)} copy(bf16[128,16,512]{2,1,0:T(8,128)(2,1)S(1)} %maximum_maximum_fusion.1) | data formatting | bytes 4194304 | tf_op jit(solution)/shard_map/concatenate | solution.py:78
  75.8 8.2 %divide_convert_fusion = bf16[512,64,128]{2,1,0:T(8,128)(2,1)} fusion(f32[]{:T(128)S(6)} %max.7, bf16[64,16,512]{0,1,2:T(8,128)(2,1)} %copy.27, bf16[128,16,512]{0,1,2:T(8,128)(2,1)} %copy.31), kind=kOutput, calls=%fused_computation | convolution fusion | flops 142606336 | bytes 11534340 | tf_op jit(solution)/shard_map/iuf,kuf->fik/dot_general | solution.py:79
  84.0 12.8 %copy.32 = bf16[512,64,128]{0,2,1:T(8,128)(2,1)} copy(bf16[512,64,128]{2,1,0:T(8,128)(2,1)} %divide_convert_fusion) | data formatting | bytes 16777216 | tf_op jit(solution)/shard_map/convert_element_type | solution.py:81
  96.8 8.3 %fusion = bf16[1,64,64,512]{3,2,1,0:T(8,128)(2,1)S(1)} fusion(bf16[512,64,2,64]{0,3,2,1:T(8,128)(2,1)} %bitcast.48, bf16[2,512,512,1]{2,1,0,3:T(8,128)(2,1)S(1)} %bitcast.50), kind=kOutput, calls=%fused_computation.5 | convolution fusion | flops 4297064448 | bytes 13631488 | tf_op jit(solution)/shard_map/dot_general | solution.py:82
  105.1 6.4 %fusion.1 = bf16[1,64,64,512]{3,2,1,0:T(8,128)(2,1)} fusion(bf16[512,64,2,64]{0,3,2,1:T(8,128)(2,1)S(1)} %bitcast.49, bf16[2,512,512,1]{2,1,0,3:T(8,128)(2,1)S(1)} %bitcast.51), kind=kOutput, calls=%fused_computation.6 | convolution fusion | flops 4297064448 | bytes 13631488 | tf_op jit(solution)/shard_map/dot_general | solution.py:82
  111.4 6.3 %maximum_bitcast_fusion = bf16[2,1,64,64,512]{4,3,2,1,0:T(8,128)(2,1)} fusion(bf16[1,64,64,512]{3,2,1,0:T(8,128)(2,1)} %fusion.1, bf16[1,64,64,512]{3,2,1,0:T(8,128)(2,1)S(1)} %fusion), kind=kLoop, calls=%fused_computation.2 | loop fusion | flops 4194304 | bytes 16777216 | tf_op jit(solution)/shard_map/broadcast_in_dim | solution.py:105
  (35 shorter events, 3.8 us)
Async XLA Ops:
  0.7 31.3 %collective-permute-start.2 = (bf16[1,8]{1,0:T(2,128)(2,1)S(1)}, bf16[1,8]{1,0:T(2,128)(2,1)S(1)}, u32[]{:S(2)}, u32[]{:S(2)}) collective-permute-start(bf16[1,8]{1,0:T(2,128)(2,1)S(1)} %get-tuple-element.18), channel_id=1, source_target_pairs={{1,0},{2,1},{3,2},{4,3},{5,4},{6,5},{7,6},{8,7},{9,8},{10,9},{11,1... | collective-permute-start | bytes 56 | tf_op jit(solution)/shard_map/ppermute | solution.py:29
  0.8 31.2 %collective-permute-start.4 = (bf16[1,8]{1,0:T(2,128)(2,1)S(1)}, bf16[1,8]{1,0:T(2,128)(2,1)S(1)}, u32[]{:S(2)}, u32[]{:S(2)}) collective-permute-start(bf16[1,8]{1,0:T(2,128)(2,1)S(1)} %get-tuple-element.18), channel_id=1, source_target_pairs={{2,0},{3,1},{4,2},{5,3},{6,4},{7,5},{8,6},{9,7},{10,8},{11,9},{12,... | collective-permute-start | bytes 56 | tf_op jit(solution)/shard_map/ppermute | solution.py:29
  7.2 11.6 %copy-start.4 = (bf16[64,8,1024]{2,1,0:T(8,128)(2,1)S(1)}, bf16[64,8,1024]{2,1,0:T(8,128)(2,1)}, u32[]{:S(2)}) copy-start(bf16[64,8,1024]{2,1,0:T(8,128)(2,1)} %param.2) | copy-start | bytes 3145732
  7.2 11.7 %slice-start = ((bf16[64,8,1024]{2,1,0:T(8,128)(2,1)}), bf16[63,8,1024]{2,1,0:T(8,128)(2,1)S(1)}, s32[]{:S(2)}) async-start(bf16[64,8,1024]{2,1,0:T(8,128)(2,1)} %param.2), calls=%async_computation | async-start | bytes 2064384 | tf_op jit(solution)/shard_map/slice | solution.py:91
  7.2 11.6 %collective-permute-start = (bf16[1,8,1024]{2,1,0:T(8,128)(2,1)S(1)}, bf16[1,8,1024]{2,1,0:T(8,128)(2,1)S(1)}, u32[]{:S(2)}, u32[]{:S(2)}) collective-permute-start(bf16[1,8,1024]{2,1,0:T(8,128)(2,1)S(1)} %slice.32), channel_id=1, source_target_pairs={{0,1},{1,2},{2,3},{3,4},{4,5},{5,6},{6,7},{7,8},{8,9},{9,10},{10,1... | collective-permute-start | bytes 49160 | tf_op jit(solution)/shard_map/ppermute | solution.py:23
  20.2 1.3 %copy-start.1 = (f32[64,8,1024]{2,1,0:T(8,128)}, f32[64,8,1024]{2,1,0:T(8,128)S(1)}, u32[]{:S(2)}) copy-start(f32[64,8,1024]{2,1,0:T(8,128)S(1)} %fusion.7) | copy-start | bytes 6291460
  24.4 1.6 %copy-start.2 = (f32[64,8,1024]{2,1,0:T(8,128)S(1)}, f32[64,8,1024]{2,1,0:T(8,128)}, u32[]{:S(2)}) copy-start(f32[64,8,1024]{2,1,0:T(8,128)} %copy-done.1) | copy-start | bytes 6291460
  26.5 5.6 %copy-start.5 = (s32[1,8]{1,0:T(1,128)S(1)}, s32[1,8]{1,0:T(1,128)}, u32[]{:S(2)}) copy-start(s32[1,8]{1,0:T(1,128)} %param.3) | copy-start | bytes 100
  26.5 18.5 %collective-permute-start.1 = (bf16[64,8,1024]{2,1,0:T(8,128)(2,1)S(1)}, bf16[64,8,1024]{2,1,0:T(8,128)(2,1)S(1)}, u32[]{:S(2)}, u32[]{:S(2)}) collective-permute-start(bf16[64,8,1024]{2,1,0:T(8,128)(2,1)S(1)} %fusion.9), channel_id=1, source_target_pairs={{1,0},{2,1},{3,2},{4,3},{5,4},{6,5},{7,6},{8,7},{9,8},{10,9},{11,1... | collective-permute-start | bytes 3145736 | tf_op jit(solution)/shard_map/ppermute | solution.py:29
  34.0 36.4 %collective-permute-start.3 = (bf16[64,8,1024]{2,1,0:T(8,128)(2,1)S(1)}, bf16[64,8,1024]{2,1,0:T(8,128)(2,1)}, u32[]{:S(2)}, u32[]{:S(2)}) collective-permute-start(bf16[64,8,1024]{2,1,0:T(8,128)(2,1)S(1)} %fusion.9), channel_id=1, source_target_pairs={{2,0},{3,1},{4,2},{5,3},{6,4},{7,5},{8,6},{9,7},{10,8},{11,9},{12,... | collective-permute-start | bytes 3145736 | tf_op jit(solution)/shard_map/ppermute | solution.py:29
  84.0 12.8 %copy-start.3 = (bf16[1024,512]{1,0:T(8,128)(2,1)S(1)}, bf16[1024,512]{1,0:T(8,128)(2,1)}, u32[]{:S(2)}) copy-start(bf16[1024,512]{1,0:T(8,128)(2,1)} %pad_maximum_fusion.1) | copy-start | bytes 3145732
  96.8 8.3 %copy-start = (bf16[512,64,128]{0,2,1:T(8,128)(2,1)S(1)}, bf16[512,64,128]{0,2,1:T(8,128)(2,1)}, u32[]{:S(2)}) copy-start(bf16[512,64,128]{0,2,1:T(8,128)(2,1)} %copy.32) | copy-start | bytes 25165828
where the time goes:
time: 119 us; the launch traced here: 118 us
  local copies, waits for them, and re-layouts  42.5 us (36%)
  matrix products  32.3 us (27%)
  other arithmetic  24.9 us (21%)
  starting transfers between devices  9.28 us (8%)
  waiting for transfers between devices  7.26 us (6%)
  between operations  1.52 us (1%)
    convert_element_type x2, local copies, waits for them, and re-layouts, correlate(): stacked = (cross / total).astype(jnp.bfloat16).reshape(FREQS, CH, 2, CH)  25.7 us
    dot_general x2, matrix products, correlate(): jnp.einsum('iuf,kuf->fik', left_side, right_side, preferred_element_type=...  16.4 us
    dot_general x2, matrix products, correlate(): lax.dot_general(stacked, inverse_parts, (((0, 2), (1, 0)), ((), ())), pre...  14.6 us
    neg x1, other arithmetic, forward_twiddles(): -jnp.sin(phase)  8.24 us
    concatenate x2, local copies, waits for them, and re-layouts, correlate(): right_side = jnp.concatenate([real_rows, imag_rows], axis=0)  7.82 us
    ppermute x4, waiting for transfers between devices, from_behind(): return lax.ppermute(block, axis, route)  7.26 us
    broadcast_in_dim x1, other arithmetic, shards(): return jnp.stack(results, axis=0)[:, None]  6.35 us
    ppermute x4, starting transfers between devices, from_behind(): return lax.ppermute(block, axis, route)  5.9 us
  transfers between devices with their start and end apart: 5, of which 1 were waited for; matrix products, arithmetic and copies ran while one was open for 41% of the time, Pallas kernels for 0%

commit v1 on v0

v1 whole, which is shorter than its diff:
```python
import functools
import math

import jax
import jax.numpy as jnp
import ml_dtypes
import numpy as np
from jax import lax
from jax.experimental import pallas as pl
from jax.experimental.pallas import tpu as pltpu
from jax.sharding import PartitionSpec as P

LAGS = 512
BAND = 64
ROUNDS = 2
EPSILON = 1e-05
F8 = 8

f32 = jnp.float32
bf16 = jnp.bfloat16
VMEM = pltpu.VMEM


def forward_table(samples):
    freqs = samples // 2
    phase = (np.arange(samples)[:, None] * np.arange(freqs)[None, :]) % samples
    phase = phase * (2.0 * math.pi / samples)
    table = np.concatenate([np.cos(phase), -np.sin(phase)], axis=1) / math.sqrt(samples)
    return table.astype(np.float32).astype(ml_dtypes.bfloat16)


def inverse_table(samples):
    freqs = samples // 2
    bins = np.arange(freqs)
    shifts = np.arange(LAGS) - LAGS // 2
    phase = (bins[:, None] * shifts[None, :]) % samples
    phase = phase * (2.0 * math.pi / samples)
    weight = np.where(bins == 0, 1.0, 2.0)[:, None] / math.sqrt(freqs)
    table = np.concatenate([weight * np.cos(phase), -weight * np.sin(phase)], axis=0)
    return table.astype(np.float32).astype(ml_dtypes.bfloat16)


def dot(a, b):
    return jnp.dot(a, b, preferred_element_type=f32)


def dot_nt(a, b):
    return lax.dot_general(a, b, (((1,), (1,)), ((), ())), preferred_element_type=f32)


def left_kernel(trace_ref, prior_ref, flag_ref, forward_ref, left_ref, *, step):
    windows, samples = trace_ref.shape[1:]
    freqs = samples // 2
    k_own = 4 * windows
    lanes = k_own * F8
    per = step // 2
    s = pl.program_id(0)
    base = s * step
    before = trace_ref[pl.ds(jnp.maximum(base - 1, 0), 1)].astype(f32)
    before = jnp.where(s == 0, prior_ref[...].astype(f32), before)
    here = trace_ref[pl.ds(base, step)].astype(f32)
    diffed = here - jnp.concatenate([before, here[:-1]], axis=0)
    diffed = diffed.reshape(step * windows, samples).astype(bf16)
    spectra = dot(diffed, forward_ref[...])
    power = spectra[:, :freqs] ** 2 + spectra[:, freqs:] ** 2
    high = power.astype(bf16)
    low = (power - high.astype(f32)).astype(bf16)
    same = (
        lax.broadcasted_iota(jnp.int32, (freqs, freqs), 0) // BAND
        == lax.broadcasted_iota(jnp.int32, (freqs, freqs), 1) // BAND
    )
    mean = jnp.where(same, 1.0 / BAND, 0.0).astype(bf16)
    level = dot(high, mean) + dot(low, mean)
    factor = lax.rsqrt(level + EPSILON).reshape(step, windows, freqs) * flag_ref[...][None, :, :1]
    factor = factor.reshape(step * windows, freqs)
    real = (spectra[:, :freqs] * factor).reshape(per, 2 * windows, freqs)
    imag = (spectra[:, freqs:] * factor).reshape(per, 2 * windows, freqs)
    rows = jnp.concatenate([real, imag], axis=1).reshape(per * k_own, freqs)
    turned = rows.astype(bf16).T
    row = lax.broadcasted_iota(jnp.int32, (per * k_own, lanes), 0)
    col = lax.broadcasted_iota(jnp.int32, (per * k_own, lanes), 1)
    keep = (
        lax.broadcasted_iota(jnp.int32, (F8, lanes), 1) % F8
        == lax.broadcasted_iota(jnp.int32, (F8, lanes), 0)
    )[None]
    for pair in range(0, per, 2):
        both = []
        for q in range(2):
            spread = jnp.where(row == (pair + q) * k_own + col // F8, 1.0, 0.0).astype(bf16)
            wide = dot(turned, spread).reshape(freqs // F8, F8, lanes)
            both.append(jnp.where(keep, wide, 0.0))
        left_ref[:, pair * F8 : (pair + 2) * F8, :] = jnp.concatenate(both, axis=1).astype(bf16)


def left_side(traces, prior, flags, forward):
    channels, windows, samples = traces.shape
    freqs = samples // 2
    step = 16
    rows = channels // 2 * F8
    lanes = 4 * windows * F8
    return pl.pallas_call(
        functools.partial(left_kernel, step=step),
        grid=(channels // step,),
        in_specs=[
            pl.BlockSpec(traces.shape, lambda s: (0, 0, 0)),
            pl.BlockSpec(prior.shape, lambda s: (0, 0, 0)),
            pl.BlockSpec(flags.shape, lambda s: (0, 0)),
            pl.BlockSpec(forward.shape, lambda s: (0, 0)),
        ],
        out_specs=pl.BlockSpec((freqs // F8, step // 2 * F8, lanes), lambda s: (0, s, 0)),
        out_shape=jax.ShapeDtypeStruct((freqs // F8, rows, lanes), bf16),
        compiler_params=pltpu.CompilerParams(vmem_limit_bytes=28 * 2**20),
        cost_estimate=pl.CostEstimate(flops=4 * 10**9, bytes_accessed=12 * 2**20, transcendentals=0),
        name="left_side",
    )(traces, prior, flags, forward)


GROUPS_STEP = 8
PAIRS_STEP = 4


def pair_kernel(
    even_ref, trace_ref, other_ref, prior_ref, flag_ref, scale_ref, left_ref, forward_ref, inverse_ref, *rest,
    cross_steps,
):
    out_ref, spectra_ref, right_ref, cross_ref = rest[-4:]
    channels, windows, samples = trace_ref.shape
    freqs = samples // 2
    s = pl.program_id(0)
    half = channels

    @pl.when(s == 0)
    def _():
        here = trace_ref[...].astype(f32)
        if other_ref is not trace_ref:
            here = jnp.where(even_ref[0] == 1, other_ref[...].astype(f32), here)
        diffed = here - jnp.concatenate([prior_ref[...].astype(f32), here[:-1]], axis=0)
        turned = jnp.swapaxes(diffed, 0, 1).reshape(windows * channels, samples).astype(bf16)
        for n in range(2):
            width = windows * channels // 2
            spectra_ref[:, n * width : (n + 1) * width] = dot_nt(
                forward_ref[...], turned[n * width : (n + 1) * width]
            )

        def band(b, _):
            start = pl.multiple_of(b * BAND, BAND)
            groups = BAND // F8
            g = pl.multiple_of(b * groups, groups)
            lane = lax.broadcasted_iota(jnp.int32, (groups, F8, 2 * half), 2) < half
            for w2 in range(windows // 2):
                at = slice(w2 * 2 * half, (w2 + 1) * 2 * half)
                re = spectra_ref[pl.ds(start, BAND), at]
                im = spectra_ref[pl.ds(freqs + start, BAND), at]
                level = jnp.sum(re * re + im * im, axis=0, keepdims=True) * (1.0 / BAND)
                factor = lax.rsqrt(level + EPSILON) * flag_ref[:, at]
                tiles = []
                for part in (re, im):
                    t = (part * factor).reshape(groups, F8, 2 * half)
                    r = pltpu.roll(t.reshape(BAND, 2 * half), half, 1).reshape(groups, F8, 2 * half)
                    p0 = jnp.concatenate([jnp.where(lane, t, 0.0), jnp.where(lane, r, 0.0)], axis=1)
                    p1 = jnp.concatenate([jnp.where(lane, 0.0, r), jnp.where(lane, 0.0, t)], axis=1)
                    tiles.append((p0, p1))
                for p in range(2):
                    for q in range(2):
                        row = ((q * 2 + p) * windows + 2 * w2) * F8
                        rows = slice(row, row + 2 * F8)
                        first = tiles[q][p]
                        second = tiles[1][p] if q == 0 else -tiles[0][p]
                        right_ref[pl.ds(g, groups), rows, : 2 * half] = first.astype(bf16)
                        right_ref[pl.ds(g, groups), rows, 2 * half :] = second.astype(bf16)
            return 0

        lax.fori_loop(0, freqs // BAND, band, 0)

    @pl.when((s >= 1) & (s < 1 + cross_steps))
    def _():
        base = (s - 1) * GROUPS_STEP

        def two(k, _):
            outs = []
            for e in range(2):
                g = 2 * k + e
                product = dot(left_ref[g], right_ref[base + g])
                outs.append(product.reshape(channels // 2, F8, 4 * half))
            both = jnp.concatenate(outs, axis=1).astype(bf16)
            f = pl.multiple_of((base + 2 * k) * F8, 2 * F8)
            cross_ref[:, pl.ds(f, 2 * F8), :] = both[:, :, : 2 * half]
            cross_ref[:, pl.ds(freqs + f, 2 * F8), :] = both[:, :, 2 * half :]
            return 0

        lax.fori_loop(0, GROUPS_STEP // 2, two, 0)

    @pl.when(s >= 1 + cross_steps)
    def _():
        base = (s - 1 - cross_steps) * PAIRS_STEP
        scale = scale_ref[0]
        for k in range(0, PAIRS_STEP, 2):
            stacked = jnp.concatenate([cross_ref[base + k], cross_ref[base + k + 1]], axis=1)
            lags = dot(inverse_ref[...], stacked) * scale
            out_ref[0, 0, 2 * k : 2 * k + 4] = lags.astype(bf16).T.reshape(4, channels, LAGS)


def correlate(round_index, even, trace, other, prior, flag_lanes, scale, left, forward_t, inverse_t, out):
    channels, windows, samples = trace.shape
    freqs = samples // 2
    cross_steps = freqs // F8 // GROUPS_STEP
    lag_steps = channels // 2 // PAIRS_STEP
    whole = lambda x: pl.BlockSpec(x.shape, lambda s: (0,) * x.ndim)
    smem = pl.BlockSpec(memory_space=pltpu.SMEM)
    operands = [even, trace, other, prior, flag_lanes, scale, left, forward_t, inverse_t]
    in_specs = [
        smem,
        whole(trace),
        whole(other),
        whole(prior),
        whole(flag_lanes),
        smem,
        pl.BlockSpec(
            (GROUPS_STEP,) + left.shape[1:], lambda s: (jnp.clip(s - 1, 0, cross_steps - 1), 0, 0)
        ),
        whole(forward_t),
        whole(inverse_t),
    ]
    aliases = {}
    if out is not None:
        operands.append(out)
        in_specs.append(pl.BlockSpec(memory_space=pl.ANY))
        aliases = {len(operands) - 1: 0}
    return pl.pallas_call(
        functools.partial(pair_kernel, cross_steps=cross_steps),
        grid=(1 + cross_steps + lag_steps,),
        in_specs=in_specs,
        out_specs=pl.BlockSpec(
            (1, 1, 2 * PAIRS_STEP, channels, LAGS),
            lambda s: (round_index, 0, jnp.maximum(s - 1 - cross_steps, 0), 0, 0),
        ),
        out_shape=jax.ShapeDtypeStruct((ROUNDS, 1, channels, channels, LAGS), bf16),
        scratch_shapes=[
            VMEM((samples, windows * channels), f32),
            VMEM((freqs // F8, 4 * windows * F8, 4 * channels), bf16),
            VMEM((channels // 2, samples, 2 * channels), bf16),
        ],
        input_output_aliases=aliases,
        compiler_params=pltpu.CompilerParams(vmem_limit_bytes=44 * 2**20),
        cost_estimate=pl.CostEstimate(flops=7 * 10**9, bytes_accessed=20 * 2**20, transcendentals=0),
        name="correlate",
    )(*operands)


def shards(traces, valid):
    size = lax.axis_size("blk")
    index = lax.axis_index("blk")
    channels, windows, samples = traces.shape
    forward = forward_table(samples)
    forward_t = jnp.asarray(np.ascontiguousarray(forward.T))
    inverse_t = jnp.asarray(np.ascontiguousarray(inverse_table(samples).T))
    forward = jnp.asarray(forward)
    even = (index % 2 == 0).astype(jnp.int32).reshape(1)

    def permute(x, route):
        return lax.ppermute(x, "blk", route)

    ring = lambda d: [((i + d) % size, i) for i in range(size)]
    first = permute(traces, ring(1))
    second = permute(traces, [((i + 2) % size, i) for i in range(1, size, 2)])
    relay = permute(first, [(i + 1, i) for i in range(0, size, 2)])
    last = traces[channels - 1 :]
    before = permute(last, [(i, i + 1) for i in range(size - 1)])
    flags = valid.astype(bf16)
    partner_flags = [permute(flags, ring(r)) for r in range(1, ROUNDS + 1)]

    own = valid.astype(f32)
    left = left_side(traces, before, jnp.broadcast_to(own.reshape(windows, 1), (windows, 128)), forward)
    out = None
    prior = last
    partners = [(first, first), (second, relay)]
    for r in range(1, ROUNDS + 1):
        far = partner_flags[r - 1].astype(f32)
        scale = 1.0 / jnp.maximum(jnp.sum(own * far, axis=1), 1.0)
        lanes = jnp.repeat(far, channels, axis=1)
        edge = (index + r) % size == 0
        here = jnp.where(edge, jnp.zeros_like(prior), prior)
        trace, other = partners[r - 1]
        out = correlate(r - 1, even, trace, other, here, lanes, scale, left, forward_t, inverse_t, out)
        prior = trace[channels - 1 :]
    return out


def solution(mesh):
    return jax.shard_map(
        shards,
        mesh=mesh,
        in_specs=(P(("days", "blk"), None, None), P(("days", "blk"), None)),
        out_specs=P(None, ("days", "blk"), None, None, None),
        check_vma=False,
    )
```

time: 119 us -> 87.4 us (0.73)
  Pallas kernels: 0 us -> 49.2 us
  local copies, waits for them, and re-layouts: 42.5 us -> 6.41 us
  matrix products: 32.3 us -> 0 us
  other arithmetic: 24.9 us -> 3.65 us
  starting transfers between devices: 9.28 us -> 19.5 us
    pallas_call x0 -> x3, Pallas kernels: none -> 49.2 us  [the longest x2 42.6 us: correlate(): pl.pallas_call(functools.partial(pair_kernel, cross_steps=cross_steps), g...]
    dot_general x5 -> x0, matrix products: 32.3 us -> none  [the longest x2 16.4 us: correlate(): jnp.einsum('iuf,kuf->fik', left_side, right_side, preferred_element_type=...]
    convert_element_type x2 -> x0, local copies, waits for them, and re-layouts: 25.7 us -> none  [correlate(): stacked = (cross / total).astype(jnp.bfloat16).reshape(FREQS, CH, 2, CH)]
    concatenate x3 -> x0, local copies, waits for them, and re-layouts: 11.3 us -> none  [the longest x2 7.82 us: correlate(): right_side = jnp.concatenate([real_rows, imag_rows], axis=0)]
    ppermute x5 -> x6, starting transfers between devices: 9.28 us -> 19.5 us  [permute(): return lax.ppermute(x, 'blk', route)]
    neg x1 -> x0, other arithmetic: 8.24 us -> none  [forward_twiddles(): -jnp.sin(phase)]
    broadcast_in_dim x1, other arithmetic: 6.35 us -> 0.82 us  [shards(): jnp.broadcast_to(own.reshape(windows, 1), (windows, 128))]
    another operation x1 -> x0, other arithmetic: 4.42 us -> none
  transfers between devices with their start and end apart: 5 -> 6, of which waited for: 1 -> 1; matrix products, arithmetic and copies ran while one was open for 41% -> 5% of each run, Pallas kernels for 0% -> 32%
where the time goes in v1:
time: 87.4 us; the launch traced here: 86.6 us
  Pallas kernels  49.2 us (56%)
  starting transfers between devices  19.5 us (22%)
  local copies, waits for them, and re-layouts  6.41 us (7%)
  waiting for transfers between devices  6.32 us (7%)
  other arithmetic  3.65 us (4%)
  between operations  1.52 us (2%)
    pallas_call x2, Pallas kernels, correlate(): pl.pallas_call(functools.partial(pair_kernel, cross_steps=cross_steps), g...  42.6 us
    ppermute x6, starting transfers between devices, permute(): return lax.ppermute(x, 'blk', route)  19.5 us
    pallas_call x1, Pallas kernels, left_side(): pl.pallas_call(functools.partial(left_kernel, step=step), grid=(channels...  6.64 us
    ppermute x6, waiting for transfers between devices, permute(): return lax.ppermute(x, 'blk', route)  6.32 us
    unnamed x10, local copies, waits for them, and re-layouts  6.05 us
  transfers between devices with their start and end apart: 6, of which 1 were waited for; matrix products, arithmetic and copies ran while one was open for 5% of the time, Pallas kernels for 32%

profile of v1, /device:TPU:1, one launch (start us, length us, event | category | flops | bytes accessed | tf_op | source)
XLA Modules:
  0.0 86.6 jit_solution(17068701278613120611)
XLA Ops:
  0.0 0.1 collective-permute-start.1
  0.1 0.8 convert_bitcast_fusion.1
  0.9 5.4 %collective-permute-start.5 = (bf16[1,8]{1,0:T(2,128)(2,1)S(1)}, bf16[1,8]{1,0:T(2,128)(2,1)S(1)}, u32[]{:S(2)}, u32[]{:S(2)}) collective-permute-start(bf16[1,8]{1,0:T(2,128)(2,1)S(1)} %get-tuple-element.10), channel_id=1, source_target_pairs={{1,0},{2,1},{3,2},{4,3},{5,4},{6,5},{7,6},{8,7},{9,8},{10,9},{11,1... | collective-permute-start | bytes 56 | tf_op jit(solution)/shard_map/ppermute | solution.py:261
  6.2 0.5 collective-permute-start.3
  6.8 2.8 %collective-permute-start = (bf16[64,8,1024]{2,1,0:T(8,128)(2,1)}, bf16[64,8,1024]{2,1,0:T(8,128)(2,1)}, u32[]{:S(2)}, u32[]{:S(2)}) collective-permute-start(bf16[64,8,1024]{2,1,0:T(8,128)(2,1)} %trace_ref.1), channel_id=1, source_target_pairs={{3,1},{5,3},{7,5},{9,7},{11,9},{13,11},{15,13},{1,15},{19,17},{21,... | collective-permute-start | bytes 3145736 | tf_op jit(solution)/shard_map/ppermute | solution.py:261
  9.6 0.8 broadcast_select_fusion
  10.3 2.8 %collective-permute-start.4 = (bf16[1,8,1024]{2,1,0:T(8,128)(2,1)S(1)}, bf16[1,8,1024]{2,1,0:T(8,128)(2,1)S(1)}, u32[]{:S(2)}, u32[]{:S(2)}) collective-permute-start(bf16[1,8,1024]{2,1,0:T(8,128)(2,1)S(1)} %get-tuple-element.8), channel_id=1, source_target_pairs={{0,1},{1,2},{2,3},{3,4},{4,5},{5,6},{6,7},{7,8},{8,9},{9,10},{10,1... | collective-permute-start | bytes 49160 | tf_op jit(solution)/shard_map/ppermute | solution.py:261
  13.1 6.3 %collective-permute-done.5 = bf16[1,8]{1,0:T(2,128)(2,1)S(1)} collective-permute-done((bf16[1,8]{1,0:T(2,128)(2,1)S(1)}, bf16[1,8]{1,0:T(2,128)(2,1)S(1)}, u32[]{:S(2)}, u32[]{:S(2)}) %collective-permute-start.5) | collective-permute-done | bytes 48 | tf_op jit(solution)/shard_map/ppermute | solution.py:261
  19.4 1.3 %multiply_reduce_fusion = (f32[]{:T(128)}, f32[]{:T(128)}) fusion(bf16[1,8]{1,0:T(2,128)(2,1)S(1)} %collective-permute-done.5, s32[1,8]{1,0:T(1,128)} %param.6, bf16[1,8]{1,0:T(2,128)(2,1)S(1)} %collective-permute-done.3), kind=kLoop, calls=%fused_computation.2 | loop fusion | flops 54 | bytes 72 | tf_op jit(solution)/shard_map/reduce_sum | solution.py:279
  20.8 0.1 broadcast_in_dim.21
  20.9 0.1 broadcast_in_dim.22.flag_ref
  22.3 0.1 broadcast_in_dim.17
  22.4 0.1 broadcast_in_dim.18.flag_ref
  22.5 0.0 collective-permute-done.1.trace_ref.other_ref
  22.5 8.0 %collective-permute-start.2 = (bf16[64,8,1024]{2,1,0:T(8,128)(2,1)}, bf16[64,8,1024]{2,1,0:T(8,128)(2,1)S(1)}, u32[]{:S(2)}, u32[]{:S(2)}) collective-permute-start(bf16[64,8,1024]{2,1,0:T(8,128)(2,1)} %collective-permute-done.1.trace_ref.other_ref), channel_id=1, source_target_pairs={{1,0},{3,2},{5,4},{7,6},{9,8},{11,10},{13,12},{15,14},{17,16},{19,... | collective-permute-start | bytes 3145736 | tf_op jit(solution)/shard_map/ppermute | solution.py:261
  30.5 0.0 collective-permute-done.4.prior_ref
  30.5 0.1 broadcast_in_dim.20.flag_ref
  30.6 1.2 %copy-done.3 = bf16[64,8,1024]{2,1,0:T(8,128)(2,1)S(1)} copy-done((bf16[64,8,1024]{2,1,0:T(8,128)(2,1)S(1)}, bf16[64,8,1024]{2,1,0:T(8,128)(2,1)}, u32[]{:S(2)}) %copy-start.3) | copy-done | bytes 1048600
  31.8 1.6 %copy-done.4 = bf16[1024,1024]{1,0:T(8,128)(2,1)S(1)} copy-done((bf16[1024,1024]{1,0:T(8,128)(2,1)S(1)}, bf16[1024,1024]{1,0:T(8,128)(2,1)}, u32[]{:S(2)}) %copy-start.4) | copy-done | bytes 2097176
  33.4 6.6 %left_side.1.left_ref = bf16[64,256,256]{2,1,0:T(8,128)(2,1)S(1)} custom-call(bf16[64,8,1024]{2,1,0:T(8,128)(2,1)S(1)} %copy-done.3, bf16[1,8,1024]{2,1,0:T(8,128)(2,1)S(1)} %collective-permute-done.4.prior_ref, f32[8,128]{1,0:T(8,128)S(1)} %broadcast_in_dim.20.flag_ref, bf16[1024,1024]{1,0:T(8,128)(2,1)S(1)} %copy-done.4), custom_call_target="tpu_custom_call" | custom-call | flops 4000000000 | bytes 12582912 | tf_op jit(solution)/shard_map/left_side/pallas_call | solution.py:101
  40.1 3.2 %copy-done = bf16[64,256,256]{2,1,0:T(8,128)(2,1)} copy-done((bf16[64,256,256]{2,1,0:T(8,128)(2,1)}, bf16[64,256,256]{2,1,0:T(8,128)(2,1)S(1)}, u32[]{:S(2)}) %copy-start) | copy-done | bytes 8388632
  43.3 0.7 slice_select_fusion.prior_ref
  44.0 21.5 %correlate.2.rest_0_ = bf16[2,1,64,64,512]{4,3,2,1,0:T(8,128)(2,1)} custom-call(s32[1]{0:T(128)} %bitcast.even_ref, bf16[64,8,1024]{2,1,0:T(8,128)(2,1)} %collective-permute-done.1.trace_ref.other_ref, bf16[64,8,1024]{2,1,0:T(8,128)(2,1)} %collective-permute-done.1.trace_ref.other_ref, bf16[1,8,1024]{2,1,0:T(8,128)(2,1)S(1)} %get-tuple-element.7.prior_ref, ...), custom_call_target="tpu_custom_call" | custom-call | flops 7000000000 | bytes 20971520 | tf_op jit(solution)/shard_map/correlate/pallas_call | solution.py:229
  65.5 21.1 %correlate.3 = bf16[2,1,64,64,512]{4,3,2,1,0:T(8,128)(2,1)} custom-call(s32[1]{0:T(128)} %bitcast.even_ref, bf16[64,8,1024]{2,1,0:T(8,128)(2,1)} %collective-permute-done.trace_ref, bf16[64,8,1024]{2,1,0:T(8,128)(2,1)S(1)} %collective-permute-done.2.other_ref, bf16[1,8,1024]{2,1,0:T(8,128)(2,1)S(1)} %slice_select_fusion.prior_ref, ...), custom_call_target="tpu_custom_call", output_to_operand_aliasing={{}: (9, {})} | custom-call | flops 7000000000 | bytes 20971520 | tf_op jit(solution)/shard_map/correlate/pallas_call | solution.py:229
  (12 shorter events, 0.0 us)
Async XLA Ops:
  0.0 44.0 %copy-start.2 = (bf16[512,1024]{1,0:T(8,128)(2,1)S(1)}, bf16[512,1024]{1,0:T(8,128)(2,1)}, u32[]{:S(2)}) copy-start(bf16[512,1024]{1,0:T(8,128)(2,1)} %constant.50.clone.inverse_ref) | copy-start | bytes 3145732
  0.0 44.0 %copy-start.1 = (bf16[1024,1024]{1,0:T(8,128)(2,1)S(1)}, bf16[1024,1024]{1,0:T(8,128)(2,1)}, u32[]{:S(2)}) copy-start(bf16[1024,1024]{1,0:T(8,128)(2,1)} %constant.49.clone.forward_ref) | copy-start | bytes 6291460
  0.0 22.5 %collective-permute-start.1 = (bf16[64,8,1024]{2,1,0:T(8,128)(2,1)}, bf16[64,8,1024]{2,1,0:T(8,128)(2,1)}, u32[]{:S(2)}, u32[]{:S(2)}) collective-permute-start(bf16[64,8,1024]{2,1,0:T(8,128)(2,1)} %trace_ref.1), channel_id=1, source_target_pairs={{1,0},{2,1},{3,2},{4,3},{5,4},{6,5},{7,6},{8,7},{9,8},{10,9},{11,1... | collective-permute-start | bytes 3145736 | tf_op jit(solution)/shard_map/ppermute | solution.py:261
  0.9 18.5 %collective-permute-start.5 = (bf16[1,8]{1,0:T(2,128)(2,1)S(1)}, bf16[1,8]{1,0:T(2,128)(2,1)S(1)}, u32[]{:S(2)}, u32[]{:S(2)}) collective-permute-start(bf16[1,8]{1,0:T(2,128)(2,1)S(1)} %get-tuple-element.10), channel_id=1, source_target_pairs={{1,0},{2,1},{3,2},{4,3},{5,4},{6,5},{7,6},{8,7},{9,8},{10,9},{11,1... | collective-permute-start | bytes 56 | tf_op jit(solution)/shard_map/ppermute | solution.py:261
  6.2 13.2 %collective-permute-start.3 = (bf16[1,8]{1,0:T(2,128)(2,1)S(1)}, bf16[1,8]{1,0:T(2,128)(2,1)S(1)}, u32[]{:S(2)}, u32[]{:S(2)}) collective-permute-start(bf16[1,8]{1,0:T(2,128)(2,1)S(1)} %get-tuple-element.10), channel_id=1, source_target_pairs={{2,0},{3,1},{4,2},{5,3},{6,4},{7,5},{8,6},{9,7},{10,8},{11,9},{12,... | collective-permute-start | bytes 56 | tf_op jit(solution)/shard_map/ppermute | solution.py:261
  6.8 58.8 %collective-permute-start = (bf16[64,8,1024]{2,1,0:T(8,128)(2,1)}, bf16[64,8,1024]{2,1,0:T(8,128)(2,1)}, u32[]{:S(2)}, u32[]{:S(2)}) collective-permute-start(bf16[64,8,1024]{2,1,0:T(8,128)(2,1)} %trace_ref.1), channel_id=1, source_target_pairs={{3,1},{5,3},{7,5},{9,7},{11,9},{13,11},{15,13},{1,15},{19,17},{21,... | collective-permute-start | bytes 3145736 | tf_op jit(solution)/shard_map/ppermute | solution.py:261
  10.3 20.2 %collective-permute-start.4 = (bf16[1,8,1024]{2,1,0:T(8,128)(2,1)S(1)}, bf16[1,8,1024]{2,1,0:T(8,128)(2,1)S(1)}, u32[]{:S(2)}, u32[]{:S(2)}) collective-permute-start(bf16[1,8,1024]{2,1,0:T(8,128)(2,1)S(1)} %get-tuple-element.8), channel_id=1, source_target_pairs={{0,1},{1,2},{2,3},{3,4},{4,5},{5,6},{6,7},{7,8},{8,9},{9,10},{10,1... | collective-permute-start | bytes 49160 | tf_op jit(solution)/shard_map/ppermute | solution.py:261
  22.5 43.0 %collective-permute-start.2 = (bf16[64,8,1024]{2,1,0:T(8,128)(2,1)}, bf16[64,8,1024]{2,1,0:T(8,128)(2,1)S(1)}, u32[]{:S(2)}, u32[]{:S(2)}) collective-permute-start(bf16[64,8,1024]{2,1,0:T(8,128)(2,1)} %collective-permute-done.1.trace_ref.other_ref), channel_id=1, source_target_pairs={{1,0},{3,2},{5,4},{7,6},{9,8},{11,10},{13,12},{15,14},{17,16},{19,... | collective-permute-start | bytes 3145736 | tf_op jit(solution)/shard_map/ppermute | solution.py:261
  30.6 1.2 %copy-start.3 = (bf16[64,8,1024]{2,1,0:T(8,128)(2,1)S(1)}, bf16[64,8,1024]{2,1,0:T(8,128)(2,1)}, u32[]{:S(2)}) copy-start(bf16[64,8,1024]{2,1,0:T(8,128)(2,1)} %trace_ref.1) | copy-start | bytes 3145732
  31.8 1.6 %copy-start.4 = (bf16[1024,1024]{1,0:T(8,128)(2,1)S(1)}, bf16[1024,1024]{1,0:T(8,128)(2,1)}, u32[]{:S(2)}) copy-start(bf16[1024,1024]{1,0:T(8,128)(2,1)} %constant.51.clone.forward_ref) | copy-start | bytes 6291460
  40.1 3.2 %copy-start = (bf16[64,256,256]{2,1,0:T(8,128)(2,1)}, bf16[64,256,256]{2,1,0:T(8,128)(2,1)S(1)}, u32[]{:S(2)}) copy-start(bf16[64,256,256]{2,1,0:T(8,128)(2,1)S(1)} %left_side.1.left_ref) | copy-start | bytes 25165828

commit v2 on v1

v2 whole, which is shorter than its diff:
```python
import functools
import math

import jax
import jax.numpy as jnp
import ml_dtypes
import numpy as np
from jax import lax
from jax.experimental import pallas as pl
from jax.experimental.pallas import tpu as pltpu
from jax.sharding import PartitionSpec as P

LAGS = 512
BAND = 64
ROUNDS = 2
EPSILON = 1e-05
F8 = 8

f32 = jnp.float32
bf16 = jnp.bfloat16
VMEM = pltpu.VMEM


def bin_order(freqs):
    bins = np.arange(freqs).reshape(-1, BAND)
    kinds = [bins[:, bins[0] % 4 == 0], bins[:, bins[0] % 4 == 2], bins[:, bins[0] % 2 == 1]]
    return np.concatenate(kinds, axis=1).reshape(-1)


def forward_table(samples):
    bins = bin_order(samples // 2)
    phase = (np.arange(samples)[:, None] * bins[None, :]) % samples
    phase = phase * (2.0 * math.pi / samples)
    table = np.concatenate([np.cos(phase), -np.sin(phase)], axis=1) / math.sqrt(samples)
    return table.astype(np.float32).astype(ml_dtypes.bfloat16)


def inverse_table(samples):
    freqs = samples // 2
    bins = np.arange(freqs)
    shifts = np.arange(LAGS) - LAGS // 2
    phase = (bins[:, None] * shifts[None, :]) % samples
    phase = phase * (2.0 * math.pi / samples)
    weight = np.where(bins == 0, 1.0, 2.0)[:, None] / math.sqrt(freqs)
    parts = [weight * np.cos(phase), -weight * np.sin(phase)]
    kinds = [bins % 4 == 0, bins % 4 == 2, bins % 2 == 1]
    table = np.concatenate([part[kind] for kind in kinds for part in parts], axis=0)
    return table.astype(np.float32).astype(ml_dtypes.bfloat16)


def dot(a, b):
    return jnp.dot(a, b, preferred_element_type=f32)


def dot_nt(a, b):
    return lax.dot_general(a, b, (((1,), (1,)), ((), ())), preferred_element_type=f32)


def dot_tn(a, b):
    return lax.dot_general(a, b, (((0,), (0,)), ((), ())), preferred_element_type=f32)


def left_kernel(trace_ref, prior_ref, forward_ref, left_ref, *, step):
    channels, windows, samples = trace_ref.shape
    channels -= 1
    freqs = samples // 2
    k_own = 4 * windows
    lanes = k_own * F8
    per = step // 2
    same = (
        lax.broadcasted_iota(jnp.int32, (freqs, freqs), 0) // BAND
        == lax.broadcasted_iota(jnp.int32, (freqs, freqs), 1) // BAND
    )
    mean = jnp.where(same, 1.0 / BAND, 0.0).astype(bf16)
    usable = trace_ref[channels, :, :freqs].astype(f32)
    row = lax.broadcasted_iota(jnp.int32, (per * k_own, lanes), 0)
    col = lax.broadcasted_iota(jnp.int32, (per * k_own, lanes), 1)
    keep = (
        lax.broadcasted_iota(jnp.int32, (F8, lanes), 1) % F8
        == lax.broadcasted_iota(jnp.int32, (F8, lanes), 0)
    )[None]

    def chunk(s, _):
        base = s * step
        before = trace_ref[pl.ds(jnp.maximum(base - 1, 0), 1)].astype(f32)
        before = jnp.where(s == 0, prior_ref[...].astype(f32), before)
        here = trace_ref[pl.ds(base, step)].astype(f32)
        diffed = here - jnp.concatenate([before, here[:-1]], axis=0)
        diffed = diffed.reshape(step * windows, samples).astype(bf16)
        spectra = dot(diffed, forward_ref[...])
        power = spectra[:, :freqs] ** 2 + spectra[:, freqs:] ** 2
        high = power.astype(bf16)
        low = (power - high.astype(f32)).astype(bf16)
        level = dot(high, mean) + dot(low, mean)
        factor = lax.rsqrt(level + EPSILON).reshape(step, windows, freqs) * usable[None]
        factor = factor.reshape(step * windows, freqs)
        real = (spectra[:, :freqs] * factor).reshape(per, 2 * windows, freqs)
        imag = (spectra[:, freqs:] * factor).reshape(per, 2 * windows, freqs)
        rows = jnp.concatenate([real, imag], axis=1).reshape(per * k_own, freqs)
        turned = rows.astype(bf16).T
        for pair in range(0, per, 2):
            both = []
            for q in range(2):
                spread = jnp.where(row == (pair + q) * k_own + col // F8, 1.0, 0.0).astype(bf16)
                wide = dot(turned, spread).reshape(freqs // F8, F8, lanes)
                both.append(jnp.where(keep, wide, 0.0))
            at = pl.multiple_of((s * per + pair) * F8, 2 * F8)
            left_ref[:, pl.ds(at, 2 * F8), :] = jnp.concatenate(both, axis=1).astype(bf16)
        return 0

    lax.fori_loop(0, channels // step, chunk, 0)


SMEM_SPEC = pl.BlockSpec(memory_space=pltpu.SMEM)
VMEM_SPEC = pl.BlockSpec(memory_space=pltpu.VMEM)


def left_side(traces, prior, forward):
    channels, windows, samples = traces.shape
    channels -= 1
    freqs = samples // 2
    return pl.pallas_call(
        functools.partial(left_kernel, step=16),
        in_specs=[VMEM_SPEC] * 3,
        out_specs=VMEM_SPEC,
        out_shape=jax.ShapeDtypeStruct((freqs // F8, channels // 2 * F8, 4 * windows * F8), bf16),
        compiler_params=pltpu.CompilerParams(vmem_limit_bytes=28 * 2**20),
        cost_estimate=pl.CostEstimate(flops=4 * 10**9, bytes_accessed=12 * 2**20, transcendentals=0),
        name="left_side",
    )(traces, prior, forward)


def pair_kernel(
    trace_ref, other_ref, own_ref, prior_ref, left_ref, forward_ref, inverse_ref, *rest,
    round_index,
):
    out_ref, spectra_ref, right_ref, cross_ref, lag_ref, sems = rest[-6:]
    channels, windows, samples = trace_ref.shape
    channels -= 1
    freqs = samples // 2
    half = channels
    size = lax.axis_size("blk")
    index = lax.axis_index("blk")

    here = trace_ref[...].astype(f32)
    if other_ref is not None:
        here = jnp.where(index % 2 == 0, other_ref[...].astype(f32), here)
    far_flags, here = here[channels], here[:channels]
    edge = lax.rem(index + round_index, size) == 0
    before = jnp.where(edge, 0.0, prior_ref[channels - 1 : channels].astype(f32))
    diffed = here - jnp.concatenate([before, here[:-1]], axis=0)
    turned = jnp.swapaxes(diffed, 0, 1).reshape(windows * channels, samples).astype(bf16)
    for n in range(2):
        width = windows * channels // 2
        spectra_ref[:, n * width : (n + 1) * width] = dot_nt(
            forward_ref[...], turned[n * width : (n + 1) * width]
        )

    first_half = lax.broadcasted_iota(jnp.int32, (1, 2 * half), 1) < half
    usable = [
        jnp.where(first_half, far_flags[w : w + 1, : 2 * half], far_flags[w + 1 : w + 2, : 2 * half])
        for w in range(0, windows, 2)
    ]

    groups = BAND // F8
    lane = lax.broadcasted_iota(jnp.int32, (groups, F8, 2 * half), 2) < half

    def whiten(b):
        start, g = b * BAND, b * groups
        for w2 in range(windows // 2):
            at = slice(w2 * 2 * half, (w2 + 1) * 2 * half)
            re = spectra_ref[start : start + BAND, at]
            im = spectra_ref[freqs + start : freqs + start + BAND, at]
            level = jnp.sum(re * re + im * im, axis=0, keepdims=True) * (1.0 / BAND)
            factor = lax.rsqrt(level + EPSILON) * usable[w2]
            tiles = []
            for part in (re, im):
                t = (part * factor).reshape(groups, F8, 2 * half)
                r = pltpu.roll(t.reshape(BAND, 2 * half), half, 1).reshape(groups, F8, 2 * half)
                p0 = jnp.concatenate([jnp.where(lane, t, 0.0), jnp.where(lane, r, 0.0)], axis=1)
                p1 = jnp.concatenate([jnp.where(lane, 0.0, r), jnp.where(lane, 0.0, t)], axis=1)
                tiles.append((p0, p1))
            for p in range(2):
                for q in range(2):
                    row = ((q * 2 + p) * windows + 2 * w2) * F8
                    rows = slice(row, row + 2 * F8)
                    first = tiles[q][p]
                    second = tiles[1][p] if q == 0 else -tiles[0][p]
                    right_ref[g : g + groups, rows, : 2 * half] = first.astype(bf16)
                    right_ref[g : g + groups, rows, 2 * half :] = second.astype(bf16)

    def cross(b):
        bands = freqs // BAND
        quarter = BAND // 4
        for pair in range(groups // 2):
            outs = []
            for e in range(2):
                g = b * groups + 2 * pair + e
                product = dot(left_ref[g], right_ref[g])
                outs.append(product.reshape(channels // 2, F8, 4 * half))
            both = jnp.concatenate(outs, axis=1).astype(bf16)
            kind = min(pair, 2)
            count = 1 if kind < 2 else 2
            row = 2 * kind * bands * quarter + (b * count + pair - kind) * quarter
            cross_ref[:, row : row + quarter, :] = both[:, :, : 2 * half]
            row += count * bands * quarter
            cross_ref[:, row : row + quarter, :] = both[:, :, 2 * half :]

    whiten(0)
    for b in range(freqs // BAND):
        if b + 1 < freqs // BAND:
            whiten(b + 1)
        cross(b)

    both_flags = own_ref[channels, :, :LAGS].astype(f32) * far_flags[:, :LAGS]
    scale = 1.0 / jnp.maximum(jnp.sum(both_flags, axis=0, keepdims=True), 1.0)

    group = 4

    def copy(k):
        at = pl.ds(k * 2 * group, 2 * group)
        return pltpu.make_async_copy(lag_ref.at[at], out_ref.at[round_index - 1, 0, at], sems.at[k])

    copies = channels // 2 // group
    quarter = samples // 4
    near = LAGS // 2

    def lags(k, _):
        for u in range(LAG_UNROLL):
            n = k * LAG_UNROLL + u
            stacked = jnp.concatenate([cross_ref[n * group + e] for e in range(group)], axis=1)
            zero = dot_tn(stacked[:quarter], inverse_ref[:quarter, :near])
            two = dot_tn(stacked[quarter : 2 * quarter], inverse_ref[quarter : 2 * quarter, :near])
            odd = dot_tn(stacked[2 * quarter :], inverse_ref[2 * quarter :, :])
            result = jnp.concatenate([zero + two + odd[:, :near], zero - two + odd[:, near:]], axis=1) * scale
            lag_ref[pl.ds(n * 2 * group, 2 * group)] = result.astype(bf16).reshape(2 * group, channels, LAGS)
            copy(n).start()
        return 0

    lax.fori_loop(0, copies // LAG_UNROLL, lags, 0)

    def finish(k, _):
        copy(k).wait()
        return 0

    lax.fori_loop(0, copies, finish, 0)


LAG_UNROLL = 4


def correlate(round_index, trace, other, own, prior, left, forward_t, inverse, out):
    channels, windows, samples = trace.shape
    channels -= 1
    freqs = samples // 2
    operands = [trace] + ([other] if other is not None else []) + [own]
    operands += ([prior] if prior is not own else []) + [left, forward_t, inverse]
    in_specs = [VMEM_SPEC] * len(operands)
    aliases = {}
    if out is not None:
        operands.append(out)
        in_specs.append(pl.BlockSpec(memory_space=pl.ANY))
        aliases = {len(operands) - 1: 0}

    def kernel(trace_ref, *refs):
        refs = list(refs)
        other_ref = refs.pop(0) if other is not None else None
        own_ref = refs.pop(0)
        prior_ref = refs.pop(0) if prior is not own else own_ref
        pair_kernel(trace_ref, other_ref, own_ref, prior_ref, *refs, round_index=round_index)

    return pl.pallas_call(
        kernel,
        in_specs=in_specs,
        out_specs=pl.BlockSpec(memory_space=pl.ANY),
        out_shape=jax.ShapeDtypeStruct((ROUNDS, 1, channels, channels, LAGS), bf16),
        scratch_shapes=[
            VMEM((samples, windows * channels), f32),
            VMEM((freqs // F8, 4 * windows * F8, 4 * channels), bf16),
            VMEM((channels // 2, samples, 2 * channels), bf16),
            VMEM((channels, channels, LAGS), bf16),
            pltpu.SemaphoreType.DMA((channels // 8,)),
        ],
        input_output_aliases=aliases,
        compiler_params=pltpu.CompilerParams(vmem_limit_bytes=32 * 2**20),
        cost_estimate=pl.CostEstimate(flops=7 * 10**9, bytes_accessed=20 * 2**20, transcendentals=0),
        name="correlate",
    )(*operands)


def shards(traces, valid):
    size = lax.axis_size("blk")
    channels, windows, samples = traces.shape
    forward = forward_table(samples)
    forward_t = jnp.asarray(np.ascontiguousarray(forward.T))
    inverse = jnp.asarray(inverse_table(samples))
    forward = jnp.asarray(forward)

    def permute(x, route):
        return lax.ppermute(x, "blk", route)

    ring = lambda d: [((i + d) % size, i) for i in range(size)]
    before = permute(traces[channels - 1 :], [(i, i + 1) for i in range(size - 1)])
    flag_row = jnp.broadcast_to(valid.astype(bf16)[:, :, None], (1, windows, samples))
    block = jnp.concatenate([traces, flag_row], axis=0)
    block, before = lax.optimization_barrier((block, before))
    first = permute(block, ring(1))
    left = left_side(block, before, forward)
    left, sent = lax.optimization_barrier((left, block))
    second = permute(sent, [((i + 2) % size, i) for i in range(1, size, 2)])
    first, left = lax.optimization_barrier((first, left))
    relay = permute(first, [(i + 1, i) for i in range(0, size, 2)])

    out = correlate(1, first, None, block, block, left, forward_t, inverse, None)
    return correlate(2, second, relay, block, first, left, forward_t, inverse, out)


def solution(mesh):
    return jax.shard_map(
        shards,
        mesh=mesh,
        in_specs=(P(("days", "blk"), None, None), P(("days", "blk"), None)),
        out_specs=P(None, ("days", "blk"), None, None, None),
        check_vma=False,
    )
```

time: 87.4 us -> 46.2 us (0.53)
  Pallas kernels: 49.2 us -> 25.7 us
  starting transfers between devices: 19.5 us -> 11.5 us
  local copies, waits for them, and re-layouts: 6.41 us -> 1.14 us
  other arithmetic: 3.65 us -> 2.13 us
  between operations: 1.52 us -> 0.27 us
  waiting for transfers between devices: 6.32 us -> 5.11 us
    pallas_call x3, Pallas kernels: 49.2 us -> 25.7 us  [the longest x2 19.2 us: correlate(): pl.pallas_call(kernel, in_specs=in_specs, out_specs=pl.BlockSpec(memory_s...]
    ppermute x6 -> x4, starting transfers between devices: 19.5 us -> 11.5 us  [permute(): return lax.ppermute(x, 'blk', route)]
    unnamed x10 -> x6, local copies, waits for them, and re-layouts: 6.05 us -> 0.35 us
    select_n x2 -> x0, other arithmetic: 1.48 us -> none  [shards(): here = jnp.where(edge, jnp.zeros_like(prior), prior)]
    concatenate x0 -> x1, other arithmetic: none -> 1.47 us  [shards(): block = jnp.concatenate([traces, flag_row], axis=0)]
    reduce_sum x1 -> x0, other arithmetic: 1.34 us -> none  [shards(): scale = 1.0 / jnp.maximum(jnp.sum(own * far, axis=1), 1.0)]
    ppermute x6 -> x4, waiting for transfers between devices: 6.32 us -> 5.11 us  [permute(): return lax.ppermute(x, 'blk', route)]
  transfers between devices with their start and end apart: 6 -> 4, of which waited for: 1 -> 1; matrix products, arithmetic and copies ran while one was open for 5% -> 5% of each run, Pallas kernels for 32% -> 35%
where the time goes in v2:
time: 46.2 us; the launch traced here: 45.8 us
  Pallas kernels  25.7 us (56%)
  starting transfers between devices  11.5 us (25%)
  waiting for transfers between devices  5.11 us (11%)
  other arithmetic  2.13 us (5%)
  local copies, waits for them, and re-layouts  1.14 us (2%)
    pallas_call x2, Pallas kernels, correlate(): pl.pallas_call(kernel, in_specs=in_specs, out_specs=pl.BlockSpec(memory_s...  19.2 us
    ppermute x4, starting transfers between devices, permute(): return lax.ppermute(x, 'blk', route)  11.5 us
    pallas_call x1, Pallas kernels, left_side(): pl.pallas_call(functools.partial(left_kernel, step=16), in_specs=[VMEM_SP...  6.51 us
    ppermute x4, waiting for transfers between devices, permute(): return lax.ppermute(x, 'blk', route)  5.11 us
    concatenate x1, other arithmetic, shards(): block = jnp.concatenate([traces, flag_row], axis=0)  1.47 us
  transfers between devices with their start and end apart: 4, of which 1 were waited for; matrix products, arithmetic and copies ran while one was open for 5% of the time, Pallas kernels for 35%

profile of v2, /device:TPU:1, one launch (start us, length us, event | category | flops | bytes accessed | tf_op | source)
XLA Modules:
  0.0 45.8 jit_solution(16156318748384013697)
XLA Ops:
  0.0 0.7 %slice.3 = bf16[1,8,1024]{2,1,0:T(8,128)(2,1)S(1)} slice(bf16[64,8,1024]{2,1,0:T(8,128)(2,1)} %param.5), slice={[63:64], [0:8], [0:1024]} | slice | bytes 32768 | tf_op jit(solution)/shard_map/slice | solution.py:303
  0.7 4.5 %collective-permute-start = (bf16[1,8,1024]{2,1,0:T(8,128)(2,1)S(1)}, bf16[1,8,1024]{2,1,0:T(8,128)(2,1)S(1)}, u32[]{:S(2)}, u32[]{:S(2)}) collective-permute-start(bf16[1,8,1024]{2,1,0:T(8,128)(2,1)S(1)} %slice.3), channel_id=1, source_target_pairs={{0,1},{1,2},{2,3},{3,4},{4,5},{5,6},{6,7},{7,8},{8,9},{9,10},{10,1... | collective-permute-start | bytes 49160 | tf_op jit(solution)/shard_map/ppermute | solution.py:300
  5.3 0.7 %convert_bitcast_fusion = bf16[8]{0:T(256)(128)(2,1)S(1)} fusion(s32[1,8]{1,0:T(1,128)} %param.6), kind=kLoop, calls=%fused_computation.1 | loop fusion | flops 8 | bytes 48 | tf_op jit(solution)/shard_map/broadcast_in_dim | solution.py:304
  5.9 0.1 broadcast_in_dim.9
  6.0 0.0 copy-start.2
  6.0 1.5 %pad_maximum_fusion.trace_ref.refs_0_.refs_1_ = bf16[65,8,1024]{2,1,0:T(8,128)(2,1)S(1)} fusion(bf16[1,8,1024]{2,1,0:T(8,128)(2,1)S(1)} %broadcast_in_dim.9, bf16[64,8,1024]{2,1,0:T(8,128)(2,1)} %param.5), kind=kLoop, calls=%fused_computation | loop fusion | flops 532480 | bytes 2129920 | tf_op jit(solution)/shard_map/concatenate | solution.py:305
  7.5 0.0 copy-start
  7.5 0.0 copy-start.1
  7.5 0.0 collective-permute-done.prior_ref
  7.5 0.1 collective-permute-start.2
  7.6 0.3 copy-done.2
  7.9 6.5 %left_side.1.refs_1_.refs_3_ = bf16[64,256,256]{2,1,0:T(8,128)(2,1)S(1)} custom-call(bf16[65,8,1024]{2,1,0:T(8,128)(2,1)S(1)} %pad_maximum_fusion.trace_ref.refs_0_.refs_1_, bf16[1,8,1024]{2,1,0:T(8,128)(2,1)S(1)} %collective-permute-done.prior_ref, bf16[1024,1024]{1,0:T(8,128)(2,1)S(1)} %copy-done.2), custom_call_target="tpu_custom_call" | custom-call | flops 4000000000 | bytes 12582912 | tf_op jit(solution)/shard_map/left_side/pallas_call | solution.py:122
  14.4 5.6 %collective-permute-start.1 = (bf16[65,8,1024]{2,1,0:T(8,128)(2,1)S(1)}, bf16[65,8,1024]{2,1,0:T(8,128)(2,1)S(1)}, u32[]{:S(2)}, u32[]{:S(2)}) collective-permute-start(bf16[65,8,1024]{2,1,0:T(8,128)(2,1)S(1)} %pad_maximum_fusion.trace_ref.refs_0_.refs_1_), channel_id=1, source_target_pairs={{3,1},{5,3},{7,5},{9,7},{11,9},{13,11},{15,13},{1,15},{19,17},{21,... | collective-permute-start | bytes 3194888 | tf_op jit(solution)/shard_map/ppermute | solution.py:300
  20.0 5.1 %collective-permute-done.2.trace_ref.refs_2_ = bf16[65,8,1024]{2,1,0:T(8,128)(2,1)S(1)} collective-permute-done((bf16[65,8,1024]{2,1,0:T(8,128)(2,1)S(1)}, bf16[65,8,1024]{2,1,0:T(8,128)(2,1)S(1)}, u32[]{:S(2)}, u32[]{:S(2)}) %collective-permute-start.2) | collective-permute-done | bytes 1064992 | tf_op jit(solution)/shard_map/ppermute | solution.py:300
  25.1 1.3 %collective-permute-start.3 = (bf16[65,8,1024]{2,1,0:T(8,128)(2,1)S(1)}, bf16[65,8,1024]{2,1,0:T(8,128)(2,1)S(1)}, u32[]{:S(2)}, u32[]{:S(2)}) collective-permute-start(bf16[65,8,1024]{2,1,0:T(8,128)(2,1)S(1)} %collective-permute-done.2.trace_ref.refs_2_), channel_id=1, source_target_pairs={{1,0},{3,2},{5,4},{7,6},{9,8},{11,10},{13,12},{15,14},{17,16},{19,... | collective-permute-start | bytes 3194888 | tf_op jit(solution)/shard_map/ppermute | solution.py:300
  26.5 0.0 copy-done
  26.5 0.0 copy-done.1
  26.5 9.5 %correlate.2.refs_6_ = bf16[2,1,64,64,512]{4,3,2,1,0:T(8,128)(2,1)} custom-call(bf16[65,8,1024]{2,1,0:T(8,128)(2,1)S(1)} %collective-permute-done.2.trace_ref.refs_2_, bf16[65,8,1024]{2,1,0:T(8,128)(2,1)S(1)} %pad_maximum_fusion.trace_ref.refs_0_.refs_1_, bf16[64,256,256]{2,1,0:T(8,128)(2,1)S(1)} %left_side.1.refs_1_.refs_3_, ...), custom_call_target="tpu_custom_call" | custom-call | flops 7000000000 | bytes 20971520 | tf_op jit(solution)/shard_map/correlate/pallas_call | solution.py:272
  36.0 0.0 collective-permute-done.1.trace_ref
  36.0 0.0 collective-permute-done.3.refs_0_
  36.1 9.6 %correlate.3 = bf16[2,1,64,64,512]{4,3,2,1,0:T(8,128)(2,1)} custom-call(bf16[65,8,1024]{2,1,0:T(8,128)(2,1)S(1)} %collective-permute-done.1.trace_ref, bf16[65,8,1024]{2,1,0:T(8,128)(2,1)S(1)} %collective-permute-done.3.refs_0_, bf16[65,8,1024]{2,1,0:T(8,128)(2,1)S(1)} %pad_maximum_fusion.trace_ref.refs_0_.refs_1_, ...), custom_call_target="tpu_custom_call", output_to_operand_aliasing={{}: (7, {})} | custom-call | flops 7000000000 | bytes 20971520 | tf_op jit(solution)/shard_map/correlate/pallas_call | solution.py:272
Async XLA Ops:
  0.7 6.8 %collective-permute-start = (bf16[1,8,1024]{2,1,0:T(8,128)(2,1)S(1)}, bf16[1,8,1024]{2,1,0:T(8,128)(2,1)S(1)}, u32[]{:S(2)}, u32[]{:S(2)}) collective-permute-start(bf16[1,8,1024]{2,1,0:T(8,128)(2,1)S(1)} %slice.3), channel_id=1, source_target_pairs={{0,1},{1,2},{2,3},{3,4},{4,5},{5,6},{6,7},{7,8},{8,9},{9,10},{10,1... | collective-permute-start | bytes 49160 | tf_op jit(solution)/shard_map/ppermute | solution.py:300
  6.0 1.9 %copy-start.2 = (bf16[1024,1024]{1,0:T(8,128)(2,1)S(1)}, bf16[1024,1024]{1,0:T(8,128)(2,1)}, u32[]{:S(2)}) copy-start(bf16[1024,1024]{1,0:T(8,128)(2,1)} %constant.8.clone.forward_ref) | copy-start | bytes 6291460
  7.5 19.0 %copy-start = (bf16[1024,1024]{1,0:T(8,128)(2,1)S(1)}, bf16[1024,1024]{1,0:T(8,128)(2,1)}, u32[]{:S(2)}) copy-start(bf16[1024,1024]{1,0:T(8,128)(2,1)} %constant.6.clone.refs_2_.refs_4_) | copy-start | bytes 6291460
  7.5 19.0 %copy-start.1 = (bf16[1024,512]{1,0:T(8,128)(2,1)S(1)}, bf16[1024,512]{1,0:T(8,128)(2,1)}, u32[]{:S(2)}) copy-start(bf16[1024,512]{1,0:T(8,128)(2,1)} %constant.7.clone.refs_3_.refs_5_) | copy-start | bytes 3145732
  7.5 17.6 %collective-permute-start.2 = (bf16[65,8,1024]{2,1,0:T(8,128)(2,1)S(1)}, bf16[65,8,1024]{2,1,0:T(8,128)(2,1)S(1)}, u32[]{:S(2)}, u32[]{:S(2)}) collective-permute-start(bf16[65,8,1024]{2,1,0:T(8,128)(2,1)S(1)} %pad_maximum_fusion.trace_ref.refs_0_.refs_1_), channel_id=1, source_target_pairs={{1,0},{2,1},{3,2},{4,3},{5,4},{6,5},{7,6},{8,7},{9,8},{10,9},{11,1... | collective-permute-start | bytes 3194888 | tf_op jit(solution)/shard_map/ppermute | solution.py:300
  14.4 21.6 %collective-permute-start.1 = (bf16[65,8,1024]{2,1,0:T(8,128)(2,1)S(1)}, bf16[65,8,1024]{2,1,0:T(8,128)(2,1)S(1)}, u32[]{:S(2)}, u32[]{:S(2)}) collective-permute-start(bf16[65,8,1024]{2,1,0:T(8,128)(2,1)S(1)} %pad_maximum_fusion.trace_ref.refs_0_.refs_1_), channel_id=1, source_target_pairs={{3,1},{5,3},{7,5},{9,7},{11,9},{13,11},{15,13},{1,15},{19,17},{21,... | collective-permute-start | bytes 3194888 | tf_op jit(solution)/shard_map/ppermute | solution.py:300
  25.1 10.9 %collective-permute-start.3 = (bf16[65,8,1024]{2,1,0:T(8,128)(2,1)S(1)}, bf16[65,8,1024]{2,1,0:T(8,128)(2,1)S(1)}, u32[]{:S(2)}, u32[]{:S(2)}) collective-permute-start(bf16[65,8,1024]{2,1,0:T(8,128)(2,1)S(1)} %collective-permute-done.2.trace_ref.refs_2_), channel_id=1, source_target_pairs={{1,0},{3,2},{5,4},{7,6},{9,8},{11,10},{13,12},{15,14},{17,16},{19,... | collective-permute-start | bytes 3194888 | tf_op jit(solution)/shard_map/ppermute | solution.py:300

commit v3 on v2

v3 whole, which is shorter than its diff:
```python
import functools
import math

import jax
import jax.numpy as jnp
import ml_dtypes
import numpy as np
from jax import lax
from jax.experimental import pallas as pl
from jax.experimental.pallas import tpu as pltpu
from jax.sharding import PartitionSpec as P

CH = 64
LAGS = 512
BAND = 64
ROUNDS = 2
EPSILON = 1e-05
F8 = 8

f32 = jnp.float32
bf16 = jnp.bfloat16
VMEM = pltpu.VMEM


def bin_order(freqs):
    bins = np.arange(freqs).reshape(-1, BAND)
    kinds = [bins[:, bins[0] % 4 == 0], bins[:, bins[0] % 4 == 2], bins[:, bins[0] % 2 == 1]]
    return np.concatenate(kinds, axis=1).reshape(-1)


def forward_table(samples):
    bins = bin_order(samples // 2)
    phase = (np.arange(samples)[:, None] * bins[None, :]) % samples
    phase = phase * (2.0 * math.pi / samples)
    table = np.concatenate([np.cos(phase), -np.sin(phase)], axis=1) / math.sqrt(samples)
    return table.astype(np.float32).astype(ml_dtypes.bfloat16)


def inverse_table(samples):
    freqs = samples // 2
    bins = np.arange(freqs)
    shifts = np.arange(LAGS) - LAGS // 2
    phase = (bins[:, None] * shifts[None, :]) % samples
    phase = phase * (2.0 * math.pi / samples)
    weight = np.where(bins == 0, 1.0, 2.0)[:, None] / math.sqrt(freqs)
    parts = [weight * np.cos(phase), -weight * np.sin(phase)]
    kinds = [bins % 4 == 0, bins % 4 == 2, bins % 2 == 1]
    table = np.concatenate([part[kind] for kind in kinds for part in parts], axis=0)
    return table.astype(np.float32).astype(ml_dtypes.bfloat16)


def dot(a, b):
    return jnp.dot(a, b, preferred_element_type=f32)


def dot_nt(a, b):
    return lax.dot_general(a, b, (((1,), (1,)), ((), ())), preferred_element_type=f32)


def dot_tn(a, b):
    return lax.dot_general(a, b, (((0,), (0,)), ((), ())), preferred_element_type=f32)


SMEM_SPEC = pl.BlockSpec(memory_space=pltpu.SMEM)
VMEM_SPEC = pl.BlockSpec(memory_space=pltpu.VMEM)
EXTRA = 16


def early_windows(windows):
    return windows * 3 // 4


def block_kernel(flag_ref, trace_ref, early_ref, late_ref, held_ref, sems, *, step):
    channels, windows, samples = trace_ref.shape
    early = early_windows(windows)

    def copy(c):
        at = pl.ds(c * step, step)
        return pltpu.make_async_copy(trace_ref.at[at], held_ref.at[at], sems.at[c])

    for c in range(channels // step):
        copy(c).start()
    last = None
    for c in range(channels // step):
        copy(c).wait()
        here = held_ref[c * step : (c + 1) * step].astype(f32)
        before = jnp.zeros_like(here[:1]) if last is None else last
        diffed = here - jnp.concatenate([before, here[:-1]], axis=0)
        last = here[step - 1 :]
        turned = jnp.swapaxes(diffed, 0, 1).astype(bf16)
        for w in range(windows):
            row = (w if w < early else w - early) * channels + c * step
            (early_ref if w < early else late_ref)[row : row + step] = turned[w]
    window = lax.broadcasted_iota(jnp.int32, (windows, samples), 0)
    flags = jnp.zeros((windows, samples), f32)
    for w in range(windows):
        flags = jnp.where(window == w, flag_ref[0, w].astype(f32), flags)
    early_ref[early * channels :] = jnp.concatenate([last[0], flags], axis=0).astype(bf16)


def travelling(flags, traces):
    channels, windows, samples = traces.shape
    step = 16
    early = early_windows(windows)
    return pl.pallas_call(
        functools.partial(block_kernel, step=step),
        in_specs=[SMEM_SPEC, pl.BlockSpec(memory_space=pl.ANY)],
        out_specs=(VMEM_SPEC,) * 2,
        out_shape=(
            jax.ShapeDtypeStruct((early * channels + EXTRA, samples), bf16),
            jax.ShapeDtypeStruct(((windows - early) * channels, samples), bf16),
        ),
        scratch_shapes=[
            VMEM(traces.shape, bf16),
            pltpu.SemaphoreType.DMA((channels // step,)),
        ],
        compiler_params=pltpu.CompilerParams(vmem_limit_bytes=52 * 2**20),
        cost_estimate=pl.CostEstimate(flops=10**10, bytes_accessed=2 * 2**20, transcendentals=0),
        name="travelling",
    )(flags, traces)


def extra_rows(piece_ref):
    extra = piece_ref[piece_ref.shape[0] - EXTRA :].astype(f32)
    return extra[: EXTRA // 2], extra[EXTRA // 2 :]


def less_before(tile, before):
    first = lax.broadcasted_iota(jnp.int32, tile.shape, 0) == 0
    tile = tile.astype(f32)
    return jnp.where(first, tile - before, tile).astype(bf16)


def left_kernel(early_ref, late_ref, before_ref, forward_ref, left_ref, block_ref, *, step, windows):
    early = early_windows(windows)
    channels = late_ref.shape[0] // (windows - early)
    samples = late_ref.shape[1]
    freqs = samples // 2
    k_own = 4 * windows
    lanes = k_own * F8
    per = step // 2
    same = (
        lax.broadcasted_iota(jnp.int32, (freqs, freqs), 0) // BAND
        == lax.broadcasted_iota(jnp.int32, (freqs, freqs), 1) // BAND
    )
    mean = jnp.where(same, 1.0 / BAND, 0.0).astype(bf16)
    before = before_ref[0].astype(f32)
    block_ref[: early * channels] = early_ref[: early * channels]
    block_ref[early * channels : windows * channels] = late_ref[...]
    block_ref[windows * channels :] = early_ref[early * channels :]
    _, flags = extra_rows(early_ref)
    usable = jnp.concatenate(
        [jnp.broadcast_to(flags[w : w + 1, :freqs], (step, freqs)) for w in range(windows)],
        axis=0,
    )
    row = lax.broadcasted_iota(jnp.int32, (2 * step * windows, lanes), 0)
    k = lax.broadcasted_iota(jnp.int32, (2 * step * windows, lanes), 1) // F8
    place = k // 4 % 2 * (step * windows) + (k // 8 * 2 + k % 2) * step + k // 2 % 2
    keep = (
        lax.broadcasted_iota(jnp.int32, (F8, lanes), 1) % F8
        == lax.broadcasted_iota(jnp.int32, (F8, lanes), 0)
    )[None]

    def chunk(s, _):
        base = s * step
        tiles = []
        for w in range(windows):
            at = (w if w < early else w - early) * channels
            tile = (early_ref if w < early else late_ref)[pl.ds(pl.multiple_of(at + base, step), step)]
            tiles.append(less_before(tile, jnp.where(s == 0, before[w : w + 1], 0.0)))
        spectra = dot_nt(jnp.concatenate(tiles, axis=0), forward_ref[...])
        power = spectra[:, :freqs] ** 2 + spectra[:, freqs:] ** 2
        high = power.astype(bf16)
        low = (power - high.astype(f32)).astype(bf16)
        level = dot(high, mean) + dot(low, mean)
        factor = lax.rsqrt(level + EPSILON) * usable
        parts = jnp.concatenate([spectra[:, :freqs] * factor, spectra[:, freqs:] * factor], axis=0)
        turned = parts.astype(bf16).T
        for pair in range(0, per, 2):
            both = []
            for q in range(2):
                spread = jnp.where(row == place + 2 * (pair + q), 1.0, 0.0).astype(bf16)
                wide = dot(turned, spread).reshape(freqs // F8, F8, lanes)
                both.append(jnp.where(keep, wide, 0.0))
            at = pl.multiple_of((s * per + pair) * F8, 2 * F8)
            left_ref[:, pl.ds(at, 2 * F8), :] = jnp.concatenate(both, axis=1).astype(bf16)
        return 0

    lax.fori_loop(0, channels // step, chunk, 0)


def left_side(early, late, before, forward, windows):
    samples = late.shape[1]
    channels = late.shape[0] // (windows - early_windows(windows))
    freqs = samples // 2
    return pl.pallas_call(
        functools.partial(left_kernel, step=16, windows=windows),
        in_specs=[VMEM_SPEC] * 4,
        out_specs=(VMEM_SPEC,) * 2,
        out_shape=(
            jax.ShapeDtypeStruct((freqs // F8, channels // 2 * F8, 4 * windows * F8), bf16),
            jax.ShapeDtypeStruct((windows * channels + EXTRA, samples), bf16),
        ),
        compiler_params=pltpu.CompilerParams(vmem_limit_bytes=28 * 2**20),
        cost_estimate=pl.CostEstimate(flops=4 * 10**9, bytes_accessed=12 * 2**20, transcendentals=0),
        name="left_side",
    )(early, late, before, forward)


def placed(index, even_rows, odd_rows):
    return odd_rows if even_rows is None else jnp.where(index % 2 == 0, even_rows, odd_rows)


def differences(rows, before, channels):
    tiles = []
    for w in range(rows.shape[0] // channels):
        tiles.append(less_before(rows[w * channels : w * channels + 16], before[w : w + 1]))
        tiles.append(rows[w * channels + 16 : (w + 1) * channels])
    return jnp.concatenate(tiles, axis=0)


def before_first(prior_ref, index, round_index):
    last, _ = extra_rows(prior_ref)
    return jnp.where(lax.rem(index + round_index, lax.axis_size("blk")) == 0, 0.0, last)


def window_pair_flags(flags, windows, half):
    first_half = lax.broadcasted_iota(jnp.int32, (1, 2 * half), 1) < half
    return [
        jnp.where(first_half, flags[w : w + 1, : 2 * half], flags[w + 1 : w + 2, : 2 * half])
        for w in range(0, windows, 2)
    ]


def whitened_pair(spectra_ref, band, at, usable):
    freqs = spectra_ref.shape[0] // 2
    start = band * BAND
    re = spectra_ref[start : start + BAND, at]
    im = spectra_ref[freqs + start : freqs + start + BAND, at]
    level = jnp.sum(re * re + im * im, axis=0, keepdims=True) * (1.0 / BAND)
    factor = lax.rsqrt(level + EPSILON) * usable
    return re * factor, im * factor


def right_kernel(odd_refs, even_refs, odd_flag_ref, even_flag_ref, prior_ref, forward_ref, right_ref, spectra_ref, *,
                 round_index, skip):
    samples = prior_ref.shape[1]
    freqs = samples // 2
    pairs = right_ref.shape[0]
    half = spectra_ref.shape[1] // (2 * pairs)
    index = lax.axis_index("blk")

    def rows_of(refs):
        rows = jnp.concatenate([ref[: ref.shape[0] // half * half] for ref in refs], axis=0)
        return rows[: 2 * pairs * half]

    here = placed(index, None if even_refs is None else rows_of(even_refs), rows_of(odd_refs))
    _, flags = extra_rows(odd_flag_ref)
    if even_flag_ref is not None:
        flags = placed(index, extra_rows(even_flag_ref)[1], flags)
    before = before_first(prior_ref, index, round_index)[skip:]
    spectra_ref[...] = dot_nt(forward_ref[...], differences(here, before, half))
    usable = window_pair_flags(flags[skip:], 2 * pairs, half)
    groups = BAND // F8
    lane = lax.broadcasted_iota(jnp.int32, (groups, F8, 2 * half), 2) < half
    for b in range(freqs // BAND):
        g = b * groups
        for w2 in range(pairs):
            tiles = []
            at = slice(w2 * 2 * half, (w2 + 1) * 2 * half)
            for part in whitened_pair(spectra_ref, b, at, usable[w2]):
                t = part.reshape(groups, F8, 2 * half)
                r = pltpu.roll(part, half, 1).reshape(groups, F8, 2 * half)
                p0 = jnp.concatenate([jnp.where(lane, t, 0.0), jnp.where(lane, r, 0.0)], axis=1)
                p1 = jnp.concatenate([jnp.where(lane, 0.0, r), jnp.where(lane, 0.0, t)], axis=1)
                tiles.append((p0.astype(bf16), p1.astype(bf16)))
            for p in range(2):
                for q in range(2):
                    rows = slice((2 * q + p) * 2 * F8, (2 * q + p + 1) * 2 * F8)
                    right_ref[w2, g : g + groups, rows, : 2 * half] = tiles[q][p]
                    right_ref[w2, g : g + groups, rows, 2 * half :] = tiles[1][p] if q == 0 else -tiles[0][p]


def right_side(round_index, mine, skip, odd, even, prior, forward_t):
    samples = prior.shape[1]
    freqs = samples // 2
    operands, places = [], []
    for array in odd + (even or []) + [prior, forward_t]:
        if not any(array is other for other in operands):
            operands.append(array)
        places.append(next(i for i, other in enumerate(operands) if other is array))
    channels = CH

    def kernel(*refs):
        named = [refs[i] for i in places]
        odd_refs = [named.pop(0) for _ in odd]
        even_refs = [named.pop(0) for _ in even or []]
        right_kernel(odd_refs[:-1], even_refs[:-1] or None, odd_refs[-1], even_refs[-1] if even else None, *named,
                     *refs[len(operands) :], round_index=round_index, skip=skip)

    return pl.pallas_call(
        kernel,
        in_specs=[VMEM_SPEC] * len(operands),
        out_specs=VMEM_SPEC,
        out_shape=jax.ShapeDtypeStruct((mine // 2, freqs // F8, 8 * F8, 4 * channels), bf16),
        scratch_shapes=[VMEM((samples, mine * channels), f32)],
        compiler_params=pltpu.CompilerParams(vmem_limit_bytes=20 * 2**20),
        cost_estimate=pl.CostEstimate(flops=2 * 10**9, bytes_accessed=5 * 2**20, transcendentals=0),
        name="right_side",
    )(*operands)


def pair_kernel(
    odd_early_ref, even_early_ref, own_ref, left_ref, right_refs, inverse_ref, *rest, round_index
):
    out_ref, cross_ref, lag_ref, sems = rest[-4:]
    channels = right_refs[0].shape[3] // 4
    samples = inverse_ref.shape[0]
    freqs = samples // 2
    half = channels
    groups = BAND // F8
    index = lax.axis_index("blk")
    _, far_flags = extra_rows(odd_early_ref)
    if even_early_ref is not None:
        far_flags = placed(index, extra_rows(even_early_ref)[1], far_flags)
    _, own_flags = extra_rows(own_ref)

    def cross(b):
        bands = freqs // BAND
        quarter = BAND // 4
        for pair in range(groups // 2):
            outs = []
            for e in range(2):
                g = b * groups + 2 * pair + e
                right = [ref[w2, g] for ref in right_refs for w2 in range(ref.shape[0])]
                product = dot(left_ref[g], jnp.concatenate(right, axis=0))
                outs.append(product.reshape(channels // 2, F8, 4 * half))
            both = jnp.concatenate(outs, axis=1).astype(bf16)
            kind = min(pair, 2)
            count = 1 if kind < 2 else 2
            row = 2 * kind * bands * quarter + (b * count + pair - kind) * quarter
            cross_ref[:, row : row + quarter, :] = both[:, :, : 2 * half]
            row += count * bands * quarter
            cross_ref[:, row : row + quarter, :] = both[:, :, 2 * half :]

    for b in range(freqs // BAND):
        cross(b)

    both_flags = own_flags[:, :LAGS] * far_flags[:, :LAGS]
    scale = 1.0 / jnp.maximum(jnp.sum(both_flags, axis=0, keepdims=True), 1.0)

    group = 4

    def copy(k):
        at = pl.ds(k * 2 * group, 2 * group)
        return pltpu.make_async_copy(lag_ref.at[at], out_ref.at[round_index - 1, 0, at], sems.at[k])

    copies = channels // 2 // group
    quarter = samples // 4
    near = LAGS // 2

    def lags(k, _):
        for u in range(LAG_UNROLL):
            n = k * LAG_UNROLL + u
            stacked = jnp.concatenate([cross_ref[n * group + e] for e in range(group)], axis=1)
            zero = dot_tn(stacked[:quarter], inverse_ref[:quarter, :near])
            two = dot_tn(stacked[quarter : 2 * quarter], inverse_ref[quarter : 2 * quarter, :near])
            odd = dot_tn(stacked[2 * quarter :], inverse_ref[2 * quarter :, :])
            result = jnp.concatenate([zero + two + odd[:, :near], zero - two + odd[:, near:]], axis=1) * scale
            lag_ref[pl.ds(n * 2 * group, 2 * group)] = result.astype(bf16).reshape(2 * group, channels, LAGS)
            copy(n).start()
        return 0

    lax.fori_loop(0, copies // LAG_UNROLL, lags, 0)

    def finish(k, _):
        copy(k).wait()
        return 0

    lax.fori_loop(0, copies, finish, 0)


LAG_UNROLL = 8


def correlate(round_index, odd, even, own, left, rights, inverse, out):
    channels = rights[0].shape[3] // 4
    samples = inverse.shape[0]
    operands = [odd] + ([even] if even is not None else []) + [own, left, *rights, inverse]
    in_specs = [VMEM_SPEC] * len(operands)
    aliases = {}
    if out is not None:
        operands.append(out)
        in_specs.append(pl.BlockSpec(memory_space=pl.ANY))
        aliases = {len(operands) - 1: 0}

    def kernel(odd_ref, *refs):
        refs = list(refs)
        even_ref = refs.pop(0) if even is not None else None
        own_ref, left_ref = refs.pop(0), refs.pop(0)
        right_refs = [refs.pop(0) for _ in rights]
        pair_kernel(odd_ref, even_ref, own_ref, left_ref, right_refs, *refs, round_index=round_index)

    return pl.pallas_call(
        kernel,
        in_specs=in_specs,
        out_specs=pl.BlockSpec(memory_space=pl.ANY),
        out_shape=jax.ShapeDtypeStruct((ROUNDS, 1, channels, channels, LAGS), bf16),
        scratch_shapes=[
            VMEM((channels // 2, samples, 2 * channels), bf16),
            VMEM((channels, channels, LAGS), bf16),
            pltpu.SemaphoreType.DMA((channels // 8,)),
        ],
        input_output_aliases=aliases,
        compiler_params=pltpu.CompilerParams(vmem_limit_bytes=20 * 2**20),
        cost_estimate=pl.CostEstimate(flops=7 * 10**9, bytes_accessed=20 * 2**20, transcendentals=0),
        name="correlate",
    )(*operands)


def shards(traces, valid):
    size = lax.axis_size("blk")
    channels, windows, samples = traces.shape
    forward_t = jnp.asarray(np.ascontiguousarray(forward_table(samples).T))
    inverse = jnp.asarray(inverse_table(samples))

    def permute(x, route):
        return lax.ppermute(x, "blk", route)

    ring = lambda d: [((i + d) % size, i) for i in range(size)]
    before = permute(traces[channels - 1 :], [(i, i + 1) for i in range(size - 1)])
    early, late = travelling(valid, traces)
    early, late, before = lax.optimization_barrier((early, late, before))
    to_odd = [((i + 2) % size, i) for i in range(1, size, 2)]
    swap = [(i ^ 1, i) for i in range(size)]
    first_early = permute(early, ring(1))
    first_late = permute(late, ring(1))
    left, block = left_side(early, late, before, forward_t, windows)
    second = permute(block, to_odd)
    first_early, left = lax.optimization_barrier((first_early, left))
    relay_early = permute(first_early, swap)
    count = early_windows(windows)
    rights = [right_side(1, count, 0, [first_early, first_early], None, early, forward_t)]
    first_late, rights = lax.optimization_barrier((first_late, rights))
    relay_late = permute(first_late, swap)
    rights += [right_side(1, windows - count, count, [first_late, first_early], None, early, forward_t)]
    out = correlate(1, first_early, None, early, left, rights, inverse, None)

    relay = [relay_early, relay_late, relay_early]
    rights = [right_side(2, windows, 0, [second, second], relay, first_early, forward_t)]
    return correlate(2, second, relay_early, early, left, rights, inverse, out)


def solution(mesh):
    return jax.shard_map(
        shards,
        mesh=mesh,
        in_specs=(P(("days", "blk"), None, None), P(("days", "blk"), None)),
        out_specs=P(None, ("days", "blk"), None, None, None),
        check_vma=False,
    )
```

time: 46.2 us -> 44.3 us (0.959)
  waiting for transfers between devices: 5.11 us -> 1.73 us
  Pallas kernels: 25.7 us -> 28.5 us
  other arithmetic: 2.13 us -> 0 us
  starting transfers between devices: 11.5 us -> 12.1 us
    pallas_call x1 -> x5, Pallas kernels: 6.51 us -> 15.3 us  [the longest x1 7.57 us: left_side(): pl.pallas_call(functools.partial(left_kernel, step=16, windows=windows),...]
    pallas_call x2, Pallas kernels: 19.2 us -> 13.2 us  [correlate(): pl.pallas_call(kernel, in_specs=in_specs, out_specs=pl.BlockSpec(memory_s...]
    ppermute x4 -> x6, waiting for transfers between devices: 5.11 us -> 1.73 us  [permute(): return lax.ppermute(x, 'blk', route)]
    concatenate x1 -> x0, other arithmetic: 1.47 us -> none  [shards(): block = jnp.concatenate([traces, flag_row], axis=0)]
    broadcast_in_dim x1 -> x0, other arithmetic: 0.66 us -> none  [shards(): jnp.broadcast_to(valid.astype(bf16)[:, :, None], (1, windows, samples))]
    ppermute x4 -> x6, starting transfers between devices: 11.5 us -> 12.1 us  [permute(): return lax.ppermute(x, 'blk', route)]
  transfers between devices with their start and end apart: 4 -> 6, of which waited for: 1 -> 1; matrix products, arithmetic and copies ran while one was open for 5% -> 0% of each run, Pallas kernels for 35% -> 44%
where the time goes in v3:
time: 44.3 us; the launch traced here: 44 us
  Pallas kernels  28.5 us (64%)
  starting transfers between devices  12.1 us (27%)
  waiting for transfers between devices  1.73 us (4%)
  local copies, waits for them, and re-layouts  1.38 us (3%)
    pallas_call x2, Pallas kernels, correlate(): pl.pallas_call(kernel, in_specs=in_specs, out_specs=pl.BlockSpec(memory_s...  13.2 us
    ppermute x6, starting transfers between devices, permute(): return lax.ppermute(x, 'blk', route)  12.1 us
    pallas_call x1, Pallas kernels, left_side(): pl.pallas_call(functools.partial(left_kernel, step=16, windows=windows),...  7.57 us
    pallas_call x3, Pallas kernels, right_side(): pl.pallas_call(kernel, in_specs=[VMEM_SPEC] * len(operands), out_specs=VM...  5.64 us
    pallas_call x1, Pallas kernels, travelling(): pl.pallas_call(functools.partial(block_kernel, step=step), in_specs=[SMEM...  2.08 us
    ppermute x6, waiting for transfers between devices, permute(): return lax.ppermute(x, 'blk', route)  1.73 us
  transfers between devices with their start and end apart: 6, of which 1 were waited for; matrix products, arithmetic and copies ran while one was open for 0% of the time, Pallas kernels for 44%

profile of v3, /device:TPU:1, one launch (start us, length us, event | category | flops | bytes accessed | tf_op | source)
XLA Modules:
  0.0 44.0 jit_solution(1381384731291610806)
XLA Ops:
  0.0 0.7 %slice.3 = bf16[1,8,1024]{2,1,0:T(8,128)(2,1)S(1)} slice(bf16[64,8,1024]{2,1,0:T(8,128)(2,1)} %trace_ref.1), slice={[63:64], [0:8], [0:1024]} | slice | bytes 32768 | tf_op jit(solution)/shard_map/slice | solution.py:431
  0.7 4.7 %collective-permute-start = (bf16[1,8,1024]{2,1,0:T(8,128)(2,1)S(1)}, bf16[1,8,1024]{2,1,0:T(8,128)(2,1)S(1)}, u32[]{:S(2)}, u32[]{:S(2)}) collective-permute-start(bf16[1,8,1024]{2,1,0:T(8,128)(2,1)S(1)} %slice.3), channel_id=1, source_target_pairs={{0,1},{1,2},{2,3},{3,4},{4,5},{5,6},{6,7},{7,8},{8,9},{9,10},{10,1... | collective-permute-start | bytes 49160 | tf_op jit(solution)/shard_map/ppermute | solution.py:428
  5.4 0.0 copy-start.2
  5.4 0.6 %copy-done.2 = s32[1,8]{1,0:T(1,128)S(1)} copy-done((s32[1,8]{1,0:T(1,128)S(1)}, s32[1,8]{1,0:T(1,128)}, u32[]{:S(2)}) %copy-start.2) | copy-done | bytes 56
  6.0 2.1 %travelling.1 = (bf16[400,1024]{1,0:T(8,128)(2,1)S(1)}, bf16[128,1024]{1,0:T(8,128)(2,1)S(1)}) custom-call(s32[1,8]{1,0:T(1,128)S(1)} %copy-done.2, bf16[64,8,1024]{2,1,0:T(8,128)(2,1)} %trace_ref.1), custom_call_target="tpu_custom_call" | custom-call | flops 10000000000 | bytes 2097152 | tf_op jit(solution)/shard_map/travelling/pallas_call | solution.py:105
  8.1 0.0 collective-permute-done.before_ref
  8.1 0.1 collective-permute-start.2
  8.2 2.2 %collective-permute-start.4 = (bf16[128,1024]{1,0:T(8,128)(2,1)S(1)}, bf16[128,1024]{1,0:T(8,128)(2,1)S(1)}, u32[]{:S(2)}, u32[]{:S(2)}) collective-permute-start(bf16[128,1024]{1,0:T(8,128)(2,1)S(1)} %get-tuple-element.19.late_ref), channel_id=1, source_target_pairs={{1,0},{2,1},{3,2},{4,3},{5,4},{6,5},{7,6},{8,7},{9,8},{10,9},{11,1... | collective-permute-start | bytes 786440 | tf_op jit(solution)/shard_map/ppermute | solution.py:428
  10.5 0.0 copy-done
  10.5 7.6 %left_side.1 = (bf16[64,256,256]{2,1,0:T(8,128)(2,1)S(1)}, bf16[528,1024]{1,0:T(8,128)(2,1)S(1)}) custom-call(bf16[400,1024]{1,0:T(8,128)(2,1)S(1)} %get-tuple-element.18.early_ref.refs_1_.refs_2_.refs_0_, bf16[128,1024]{1,0:T(8,128)(2,1)S(1)} %get-tuple-element.19.late_ref, bf16[1,8,1024]{2,1,0:T(8,128)(2,1)S(1)} %collective-permute-done.before_ref, ...), custom_call_target="tpu_custom_call" | custom-call | flops 4000000000 | bytes 12582912 | tf_op jit(solution)/shard_map/left_side/pallas_call | solution.py:196
  18.0 4.6 %collective-permute-start.1 = (bf16[528,1024]{1,0:T(8,128)(2,1)S(1)}, bf16[528,1024]{1,0:T(8,128)(2,1)S(1)}, u32[]{:S(2)}, u32[]{:S(2)}) collective-permute-start(bf16[528,1024]{1,0:T(8,128)(2,1)S(1)} %get-tuple-element.21), channel_id=1, source_target_pairs={{3,1},{5,3},{7,5},{9,7},{11,9},{13,11},{15,13},{1,15},{19,17},{21,... | collective-permute-start | bytes 3244040 | tf_op jit(solution)/shard_map/ppermute | solution.py:428
  22.6 0.0 collective-permute-done.2.refs_0_.refs_3_.refs_1_.odd_ref
  22.6 0.0 copy-start.1
  22.6 0.1 collective-permute-start.3
  22.7 2.1 %right_side.3.refs_2_ = bf16[3,64,64,256]{3,2,1,0:T(8,128)(2,1)S(1)} custom-call(bf16[400,1024]{1,0:T(8,128)(2,1)S(1)} %collective-permute-done.2.refs_0_.refs_3_.refs_1_.odd_ref, bf16[400,1024]{1,0:T(8,128)(2,1)S(1)} %get-tuple-element.18.early_ref.refs_1_.refs_2_.refs_0_, bf16[1024,1024]{1,0:T(8,128)(2,1)S(1)} %copy-done), custom_call_target="tpu_custom_call" | custom-call | flops 2000000000 | bytes 5242880 | tf_op jit(solution)/shard_map/right_side/pallas_call | solution.py:301
  24.8 0.0 collective-permute-done.4.refs_0_
  24.9 0.6 %collective-permute-start.5 = (bf16[128,1024]{1,0:T(8,128)(2,1)S(1)}, bf16[128,1024]{1,0:T(8,128)(2,1)S(1)}, u32[]{:S(2)}, u32[]{:S(2)}) collective-permute-start(bf16[128,1024]{1,0:T(8,128)(2,1)S(1)} %collective-permute-done.4.refs_0_), channel_id=1, source_target_pairs={{1,0},{0,1},{3,2},{2,3},{5,4},{4,5},{7,6},{6,7},{9,8},{8,9},{11,10... | collective-permute-start | bytes 786440 | tf_op jit(solution)/shard_map/ppermute | solution.py:428
  25.4 0.9 %right_side.5.refs_3_ = bf16[1,64,64,256]{3,2,1,0:T(8,128)(2,1)S(1)} custom-call(bf16[128,1024]{1,0:T(8,128)(2,1)S(1)} %collective-permute-done.4.refs_0_, bf16[400,1024]{1,0:T(8,128)(2,1)S(1)} %collective-permute-done.2.refs_0_.refs_3_.refs_1_.odd_ref, bf16[400,1024]{1,0:T(8,128)(2,1)S(1)} %get-tuple-element.18.early_ref.refs_1_.refs_2_.refs_0_, ...), custom_call_target="tpu_custom_call" | custom-call | flops 2000000000 | bytes 5242880 | tf_op jit(solution)/shard_map/right_side/pallas_call | solution.py:301
  26.4 6.6 %correlate.2.refs_5_ = bf16[2,1,64,64,512]{4,3,2,1,0:T(8,128)(2,1)} custom-call(bf16[400,1024]{1,0:T(8,128)(2,1)S(1)} %collective-permute-done.2.refs_0_.refs_3_.refs_1_.odd_ref, bf16[400,1024]{1,0:T(8,128)(2,1)S(1)} %get-tuple-element.18.early_ref.refs_1_.refs_2_.refs_0_, bf16[64,256,256]{2,1,0:T(8,128)(2,1)S(1)} %get-tuple-element.24.refs_1_.refs_2_, ...), custom_call_target="tpu_custom_call" | custom-call | flops 7000000000 | bytes 20971520 | tf_op jit(solution)/shard_map/correlate/pallas_call | solution.py:404
  32.9 1.7 %collective-permute-done.1.refs_0_.odd_ref = bf16[528,1024]{1,0:T(8,128)(2,1)S(1)} collective-permute-done((bf16[528,1024]{1,0:T(8,128)(2,1)S(1)}, bf16[528,1024]{1,0:T(8,128)(2,1)S(1)}, u32[]{:S(2)}, u32[]{:S(2)}) %collective-permute-start.1) | collective-permute-done | bytes 1081376 | tf_op jit(solution)/shard_map/ppermute | solution.py:428
  34.7 0.0 collective-permute-done.5.refs_2_
  34.7 0.0 collective-permute-done.3.refs_1_.refs_0_
  34.7 2.6 %right_side.4.refs_3_ = bf16[4,64,64,256]{3,2,1,0:T(8,128)(2,1)S(1)} custom-call(bf16[528,1024]{1,0:T(8,128)(2,1)S(1)} %collective-permute-done.1.refs_0_.odd_ref, bf16[400,1024]{1,0:T(8,128)(2,1)S(1)} %collective-permute-done.3.refs_1_.refs_0_, bf16[128,1024]{1,0:T(8,128)(2,1)S(1)} %collective-permute-done.5.refs_2_, ...), custom_call_target="tpu_custom_call" | custom-call | flops 2000000000 | bytes 5242880 | tf_op jit(solution)/shard_map/right_side/pallas_call | solution.py:301
  37.3 6.6 %correlate.3 = bf16[2,1,64,64,512]{4,3,2,1,0:T(8,128)(2,1)} custom-call(bf16[528,1024]{1,0:T(8,128)(2,1)S(1)} %collective-permute-done.1.refs_0_.odd_ref, bf16[400,1024]{1,0:T(8,128)(2,1)S(1)} %collective-permute-done.3.refs_1_.refs_0_, bf16[400,1024]{1,0:T(8,128)(2,1)S(1)} %get-tuple-element.18.early_ref.refs_1_.refs_2_.refs_0_, ...), custom_call_target="tpu_custom_call", output_to_operand_aliasing={{}: (6, {})} | custom-call | flops 7000000000 | bytes 20971520 | tf_op jit(solution)/shard_map/correlate/pallas_call | solution.py:404
  (2 shorter events, 0.0 us)
Async XLA Ops:
  0.7 9.7 %copy-start = (bf16[1024,1024]{1,0:T(8,128)(2,1)S(1)}, bf16[1024,1024]{1,0:T(8,128)(2,1)}, u32[]{:S(2)}) copy-start(bf16[1024,1024]{1,0:T(8,128)(2,1)} %constant.4.clone.forward_ref.refs_2_.refs_4_.refs_3_) | copy-start | bytes 6291460
  0.7 7.4 %collective-permute-start = (bf16[1,8,1024]{2,1,0:T(8,128)(2,1)S(1)}, bf16[1,8,1024]{2,1,0:T(8,128)(2,1)S(1)}, u32[]{:S(2)}, u32[]{:S(2)}) collective-permute-start(bf16[1,8,1024]{2,1,0:T(8,128)(2,1)S(1)} %slice.3), channel_id=1, source_target_pairs={{0,1},{1,2},{2,3},{3,4},{4,5},{5,6},{6,7},{7,8},{8,9},{9,10},{10,1... | collective-permute-start | bytes 49160 | tf_op jit(solution)/shard_map/ppermute | solution.py:428
  5.4 0.7 %copy-start.2 = (s32[1,8]{1,0:T(1,128)S(1)}, s32[1,8]{1,0:T(1,128)}, u32[]{:S(2)}) copy-start(s32[1,8]{1,0:T(1,128)} %flag_ref.1) | copy-start | bytes 100
  8.1 14.5 %collective-permute-start.2 = (bf16[400,1024]{1,0:T(8,128)(2,1)S(1)}, bf16[400,1024]{1,0:T(8,128)(2,1)S(1)}, u32[]{:S(2)}, u32[]{:S(2)}) collective-permute-start(bf16[400,1024]{1,0:T(8,128)(2,1)S(1)} %get-tuple-element.18.early_ref.refs_1_.refs_2_.refs_0_), channel_id=1, source_target_pairs={{1,0},{2,1},{3,2},{4,3},{5,4},{6,5},{7,6},{8,7},{9,8},{10,9},{11,1... | collective-permute-start | bytes 2457608 | tf_op jit(solution)/shard_map/ppermute | solution.py:428
  8.2 16.6 %collective-permute-start.4 = (bf16[128,1024]{1,0:T(8,128)(2,1)S(1)}, bf16[128,1024]{1,0:T(8,128)(2,1)S(1)}, u32[]{:S(2)}, u32[]{:S(2)}) collective-permute-start(bf16[128,1024]{1,0:T(8,128)(2,1)S(1)} %get-tuple-element.19.late_ref), channel_id=1, source_target_pairs={{1,0},{2,1},{3,2},{4,3},{5,4},{6,5},{7,6},{8,7},{9,8},{10,9},{11,1... | collective-permute-start | bytes 786440 | tf_op jit(solution)/shard_map/ppermute | solution.py:428
  18.0 16.6 %collective-permute-start.1 = (bf16[528,1024]{1,0:T(8,128)(2,1)S(1)}, bf16[528,1024]{1,0:T(8,128)(2,1)S(1)}, u32[]{:S(2)}, u32[]{:S(2)}) collective-permute-start(bf16[528,1024]{1,0:T(8,128)(2,1)S(1)} %get-tuple-element.21), channel_id=1, source_target_pairs={{3,1},{5,3},{7,5},{9,7},{11,9},{13,11},{15,13},{1,15},{19,17},{21,... | collective-permute-start | bytes 3244040 | tf_op jit(solution)/shard_map/ppermute | solution.py:428
  22.6 3.7 %copy-start.1 = (bf16[1024,512]{1,0:T(8,128)(2,1)S(1)}, bf16[1024,512]{1,0:T(8,128)(2,1)}, u32[]{:S(2)}) copy-start(bf16[1024,512]{1,0:T(8,128)(2,1)} %constant.5.clone.refs_4_) | copy-start | bytes 3145732
  22.6 12.1 %collective-permute-start.3 = (bf16[400,1024]{1,0:T(8,128)(2,1)S(1)}, bf16[400,1024]{1,0:T(8,128)(2,1)S(1)}, u32[]{:S(2)}, u32[]{:S(2)}) collective-permute-start(bf16[400,1024]{1,0:T(8,128)(2,1)S(1)} %collective-permute-done.2.refs_0_.refs_3_.refs_1_.odd_ref), channel_id=1, source_target_pairs={{1,0},{0,1},{3,2},{2,3},{5,4},{4,5},{7,6},{6,7},{9,8},{8,9},{11,10... | collective-permute-start | bytes 2457608 | tf_op jit(solution)/shard_map/ppermute | solution.py:428
  24.9 9.8 %collective-permute-start.5 = (bf16[128,1024]{1,0:T(8,128)(2,1)S(1)}, bf16[128,1024]{1,0:T(8,128)(2,1)S(1)}, u32[]{:S(2)}, u32[]{:S(2)}) collective-permute-start(bf16[128,1024]{1,0:T(8,128)(2,1)S(1)} %collective-permute-done.4.refs_0_), channel_id=1, source_target_pairs={{1,0},{0,1},{3,2},{2,3},{5,4},{4,5},{7,6},{6,7},{9,8},{8,9},{11,10... | collective-permute-start | bytes 786440 | tf_op jit(solution)/shard_map/ppermute | solution.py:428

commit v4 on v3

--- a/solution.py
+++ b/solution.py
@@ -70,7 +70,7 @@
     return windows * 3 // 4
 
 
-def block_kernel(flag_ref, trace_ref, early_ref, late_ref, held_ref, sems, *, step):
+def block_kernel(flag_ref, trace_ref, early_ref, late_ref, held_ref, held_flag_ref, sems, flag_sem, *, step):
     channels, windows, samples = trace_ref.shape
     early = early_windows(windows)
 
@@ -78,8 +78,10 @@
         at = pl.ds(c * step, step)
         return pltpu.make_async_copy(trace_ref.at[at], held_ref.at[at], sems.at[c])
 
+    flag_copy = pltpu.make_async_copy(flag_ref, held_flag_ref, flag_sem)
     for c in range(channels // step):
         copy(c).start()
+    flag_copy.start()
     last = None
     for c in range(channels // step):
         copy(c).wait()
@@ -91,10 +93,11 @@
         for w in range(windows):
             row = (w if w < early else w - early) * channels + c * step
             (early_ref if w < early else late_ref)[row : row + step] = turned[w]
+    flag_copy.wait()
     window = lax.broadcasted_iota(jnp.int32, (windows, samples), 0)
     flags = jnp.zeros((windows, samples), f32)
     for w in range(windows):
-        flags = jnp.where(window == w, flag_ref[0, w].astype(f32), flags)
+        flags = jnp.where(window == w, held_flag_ref[0, w].astype(f32), flags)
     early_ref[early * channels :] = jnp.concatenate([last[0], flags], axis=0).astype(bf16)
 
 
@@ -104,7 +107,7 @@
     early = early_windows(windows)
     return pl.pallas_call(
         functools.partial(block_kernel, step=step),
-        in_specs=[SMEM_SPEC, pl.BlockSpec(memory_space=pl.ANY)],
+        in_specs=[pl.BlockSpec(memory_space=pltpu.HBM)] * 2,
         out_specs=(VMEM_SPEC,) * 2,
         out_shape=(
             jax.ShapeDtypeStruct((early * channels + EXTRA, samples), bf16),
@@ -112,7 +115,9 @@
         ),
         scratch_shapes=[
             VMEM(traces.shape, bf16),
+            pltpu.SMEM(flags.shape, flags.dtype),
             pltpu.SemaphoreType.DMA((channels // step,)),
+            pltpu.SemaphoreType.DMA,
         ],
         compiler_params=pltpu.CompilerParams(vmem_limit_bytes=52 * 2**20),
         cost_estimate=pl.CostEstimate(flops=10**10, bytes_accessed=2 * 2**20, transcendentals=0),
@@ -202,7 +207,7 @@
             jax.ShapeDtypeStruct((windows * channels + EXTRA, samples), bf16),
         ),
         compiler_params=pltpu.CompilerParams(vmem_limit_bytes=28 * 2**20),
-        cost_estimate=pl.CostEstimate(flops=4 * 10**9, bytes_accessed=12 * 2**20, transcendentals=0),
+        cost_estimate=pl.CostEstimate(flops=10**11, bytes_accessed=12 * 2**20, transcendentals=0),
         name="left_side",
     )(early, late, before, forward)
 
@@ -428,13 +433,14 @@
         return lax.ppermute(x, "blk", route)
 
     ring = lambda d: [((i + d) % size, i) for i in range(size)]
-    before = permute(traces[channels - 1 :], [(i, i + 1) for i in range(size - 1)])
+    last, traces = lax.optimization_barrier((traces[channels - 1 :], traces))
+    before = permute(last, [(i, i + 1) for i in range(size - 1)])
     early, late = travelling(valid, traces)
-    early, late, before = lax.optimization_barrier((early, late, before))
     to_odd = [((i + 2) % size, i) for i in range(1, size, 2)]
     swap = [(i ^ 1, i) for i in range(size)]
     first_early = permute(early, ring(1))
-    first_late = permute(late, ring(1))
+    before, late_sent = lax.optimization_barrier((before, late))
+    first_late = permute(late_sent, ring(1))
     left, block = left_side(early, late, before, forward_t, windows)
     second = permute(block, to_odd)
     first_early, left = lax.optimization_barrier((first_early, left))

time: 44.3 us -> 43.8 us (0.989)
  Pallas kernels: 28.5 us -> 28 us
    pallas_call x1, Pallas kernels: 2.08 us -> 1.56 us  [travelling(): pl.pallas_call(functools.partial(block_kernel, step=step), in_specs=[pl.B...]
  transfers between devices with their start and end apart: 6 -> 6, of which waited for: 1 -> 1; matrix products, arithmetic and copies ran while one was open for 0% -> 0% of each run, Pallas kernels for 44% -> 43%
where the time goes in v4:
time: 43.8 us; the launch traced here: 43.5 us
  Pallas kernels  28 us (64%)
  starting transfers between devices  12.1 us (28%)
  waiting for transfers between devices  1.72 us (4%)
  local copies, waits for them, and re-layouts  1.38 us (3%)
    pallas_call x2, Pallas kernels, correlate(): pl.pallas_call(kernel, in_specs=in_specs, out_specs=pl.BlockSpec(memory_s...  13.2 us
    ppermute x6, starting transfers between devices, permute(): return lax.ppermute(x, 'blk', route)  12.1 us
    pallas_call x1, Pallas kernels, left_side(): pl.pallas_call(functools.partial(left_kernel, step=16, windows=windows),...  7.57 us
    pallas_call x3, Pallas kernels, right_side(): pl.pallas_call(kernel, in_specs=[VMEM_SPEC] * len(operands), out_specs=VM...  5.64 us
    ppermute x6, waiting for transfers between devices, permute(): return lax.ppermute(x, 'blk', route)  1.72 us
    pallas_call x1, Pallas kernels, travelling(): pl.pallas_call(functools.partial(block_kernel, step=step), in_specs=[pl.B...  1.56 us
  transfers between devices with their start and end apart: 6, of which 1 were waited for; matrix products, arithmetic and copies ran while one was open for 0% of the time, Pallas kernels for 43%

profile of v4, /device:TPU:1, one launch (start us, length us, event | category | flops | bytes accessed | tf_op | source)
XLA Modules:
  0.0 43.5 jit_solution(14080054071824354318)
XLA Ops:
  0.0 0.7 %slice.3 = bf16[1,8,1024]{2,1,0:T(8,128)(2,1)S(1)} slice(bf16[64,8,1024]{2,1,0:T(8,128)(2,1)} %trace_ref), slice={[63:64], [0:8], [0:1024]} | slice | bytes 32768 | tf_op jit(solution)/shard_map/slice | solution.py:436
  0.7 4.7 %collective-permute-start = (bf16[1,8,1024]{2,1,0:T(8,128)(2,1)S(1)}, bf16[1,8,1024]{2,1,0:T(8,128)(2,1)S(1)}, u32[]{:S(2)}, u32[]{:S(2)}) collective-permute-start(bf16[1,8,1024]{2,1,0:T(8,128)(2,1)S(1)} %slice.3), channel_id=1, source_target_pairs={{0,1},{1,2},{2,3},{3,4},{4,5},{5,6},{6,7},{7,8},{8,9},{9,10},{10,1... | collective-permute-start | bytes 49160 | tf_op jit(solution)/shard_map/ppermute | solution.py:433
  5.4 0.0 copy-start.2
  5.4 0.6 %copy-done.2 = s32[1,8]{1,0:T(1,128)S(1)} copy-done((s32[1,8]{1,0:T(1,128)S(1)}, s32[1,8]{1,0:T(1,128)}, u32[]{:S(2)}) %copy-start.2) | copy-done | bytes 56
  6.0 1.6 %travelling.1 = (bf16[400,1024]{1,0:T(8,128)(2,1)S(1)}, bf16[128,1024]{1,0:T(8,128)(2,1)S(1)}) custom-call(s32[1,8]{1,0:T(1,128)S(1)} %copy-done.2, bf16[64,8,1024]{2,1,0:T(8,128)(2,1)} %trace_ref), custom_call_target="tpu_custom_call" | custom-call | flops 10000000000 | bytes 2097152 | tf_op jit(solution)/shard_map/travelling/pallas_call | solution.py:108
  7.6 0.1 collective-permute-start.2
  7.7 0.0 collective-permute-done.before_ref
  7.7 2.2 %collective-permute-start.4 = (bf16[128,1024]{1,0:T(8,128)(2,1)S(1)}, bf16[128,1024]{1,0:T(8,128)(2,1)S(1)}, u32[]{:S(2)}, u32[]{:S(2)}) collective-permute-start(bf16[128,1024]{1,0:T(8,128)(2,1)S(1)} %get-tuple-element.26.late_ref), channel_id=1, source_target_pairs={{1,0},{2,1},{3,2},{4,3},{5,4},{6,5},{7,6},{8,7},{9,8},{10,9},{11,1... | collective-permute-start | bytes 786440 | tf_op jit(solution)/shard_map/ppermute | solution.py:433
  9.9 7.6 %left_side.1 = (bf16[64,256,256]{2,1,0:T(8,128)(2,1)S(1)}, bf16[528,1024]{1,0:T(8,128)(2,1)S(1)}) custom-call(bf16[400,1024]{1,0:T(8,128)(2,1)S(1)} %get-tuple-element.18.early_ref.refs_1_.refs_2_.refs_0_, bf16[128,1024]{1,0:T(8,128)(2,1)S(1)} %get-tuple-element.26.late_ref, bf16[1,8,1024]{2,1,0:T(8,128)(2,1)S(1)} %collective-permute-done.before_ref, ...), custom_call_target="tpu_custom_call" | custom-call | flops 99999997952 | bytes 12582912 | tf_op jit(solution)/shard_map/left_side/pallas_call | solution.py:201
  17.5 4.6 %collective-permute-start.1 = (bf16[528,1024]{1,0:T(8,128)(2,1)S(1)}, bf16[528,1024]{1,0:T(8,128)(2,1)S(1)}, u32[]{:S(2)}, u32[]{:S(2)}) collective-permute-start(bf16[528,1024]{1,0:T(8,128)(2,1)S(1)} %get-tuple-element.22), channel_id=1, source_target_pairs={{3,1},{5,3},{7,5},{9,7},{11,9},{13,11},{15,13},{1,15},{19,17},{21,... | collective-permute-start | bytes 3244040 | tf_op jit(solution)/shard_map/ppermute | solution.py:433
  22.1 0.0 collective-permute-done.2.refs_0_.refs_3_.refs_1_.odd_ref
  22.1 0.0 copy-start.1
  22.1 0.1 collective-permute-start.3
  22.2 2.1 %right_side.3.refs_2_ = bf16[3,64,64,256]{3,2,1,0:T(8,128)(2,1)S(1)} custom-call(bf16[400,1024]{1,0:T(8,128)(2,1)S(1)} %collective-permute-done.2.refs_0_.refs_3_.refs_1_.odd_ref, bf16[400,1024]{1,0:T(8,128)(2,1)S(1)} %get-tuple-element.18.early_ref.refs_1_.refs_2_.refs_0_, bf16[1024,1024]{1,0:T(8,128)(2,1)S(1)} %copy-done), custom_call_target="tpu_custom_call" | custom-call | flops 2000000000 | bytes 5242880 | tf_op jit(solution)/shard_map/right_side/pallas_call | solution.py:306
  24.3 0.0 collective-permute-done.4.refs_0_
  24.3 0.6 %collective-permute-start.5 = (bf16[128,1024]{1,0:T(8,128)(2,1)S(1)}, bf16[128,1024]{1,0:T(8,128)(2,1)S(1)}, u32[]{:S(2)}, u32[]{:S(2)}) collective-permute-start(bf16[128,1024]{1,0:T(8,128)(2,1)S(1)} %collective-permute-done.4.refs_0_), channel_id=1, source_target_pairs={{1,0},{0,1},{3,2},{2,3},{5,4},{4,5},{7,6},{6,7},{9,8},{8,9},{11,10... | collective-permute-start | bytes 786440 | tf_op jit(solution)/shard_map/ppermute | solution.py:433
  24.9 0.9 %right_side.5.refs_3_ = bf16[1,64,64,256]{3,2,1,0:T(8,128)(2,1)S(1)} custom-call(bf16[128,1024]{1,0:T(8,128)(2,1)S(1)} %collective-permute-done.4.refs_0_, bf16[400,1024]{1,0:T(8,128)(2,1)S(1)} %collective-permute-done.2.refs_0_.refs_3_.refs_1_.odd_ref, bf16[400,1024]{1,0:T(8,128)(2,1)S(1)} %get-tuple-element.18.early_ref.refs_1_.refs_2_.refs_0_, ...), custom_call_target="tpu_custom_call" | custom-call | flops 2000000000 | bytes 5242880 | tf_op jit(solution)/shard_map/right_side/pallas_call | solution.py:306
  25.8 0.0 copy-done.1
  25.8 6.6 %correlate.2.refs_5_ = bf16[2,1,64,64,512]{4,3,2,1,0:T(8,128)(2,1)} custom-call(bf16[400,1024]{1,0:T(8,128)(2,1)S(1)} %collective-permute-done.2.refs_0_.refs_3_.refs_1_.odd_ref, bf16[400,1024]{1,0:T(8,128)(2,1)S(1)} %get-tuple-element.18.early_ref.refs_1_.refs_2_.refs_0_, bf16[64,256,256]{2,1,0:T(8,128)(2,1)S(1)} %get-tuple-element.25.refs_1_.refs_2_, ...), custom_call_target="tpu_custom_call" | custom-call | flops 7000000000 | bytes 20971520 | tf_op jit(solution)/shard_map/correlate/pallas_call | solution.py:409
  32.4 0.0 collective-permute-done.5.refs_2_
  32.4 1.7 %collective-permute-done.1.refs_0_.odd_ref = bf16[528,1024]{1,0:T(8,128)(2,1)S(1)} collective-permute-done((bf16[528,1024]{1,0:T(8,128)(2,1)S(1)}, bf16[528,1024]{1,0:T(8,128)(2,1)S(1)}, u32[]{:S(2)}, u32[]{:S(2)}) %collective-permute-start.1) | collective-permute-done | bytes 1081376 | tf_op jit(solution)/shard_map/ppermute | solution.py:433
  34.1 0.0 collective-permute-done.3.refs_1_.refs_0_
  34.1 2.6 %right_side.4.refs_3_ = bf16[4,64,64,256]{3,2,1,0:T(8,128)(2,1)S(1)} custom-call(bf16[528,1024]{1,0:T(8,128)(2,1)S(1)} %collective-permute-done.1.refs_0_.odd_ref, bf16[400,1024]{1,0:T(8,128)(2,1)S(1)} %collective-permute-done.3.refs_1_.refs_0_, bf16[128,1024]{1,0:T(8,128)(2,1)S(1)} %collective-permute-done.5.refs_2_, ...), custom_call_target="tpu_custom_call" | custom-call | flops 2000000000 | bytes 5242880 | tf_op jit(solution)/shard_map/right_side/pallas_call | solution.py:306
  36.7 6.6 %correlate.3 = bf16[2,1,64,64,512]{4,3,2,1,0:T(8,128)(2,1)} custom-call(bf16[528,1024]{1,0:T(8,128)(2,1)S(1)} %collective-permute-done.1.refs_0_.odd_ref, bf16[400,1024]{1,0:T(8,128)(2,1)S(1)} %collective-permute-done.3.refs_1_.refs_0_, bf16[400,1024]{1,0:T(8,128)(2,1)S(1)} %get-tuple-element.18.early_ref.refs_1_.refs_2_.refs_0_, ...), custom_call_target="tpu_custom_call", output_to_operand_aliasing={{}: (6, {})} | custom-call | flops 7000000000 | bytes 20971520 | tf_op jit(solution)/shard_map/correlate/pallas_call | solution.py:409
  (2 shorter events, 0.0 us)
Async XLA Ops:
  0.7 9.2 %copy-start = (bf16[1024,1024]{1,0:T(8,128)(2,1)S(1)}, bf16[1024,1024]{1,0:T(8,128)(2,1)}, u32[]{:S(2)}) copy-start(bf16[1024,1024]{1,0:T(8,128)(2,1)} %constant.4.clone.forward_ref.refs_2_.refs_4_.refs_3_) | copy-start | bytes 6291460
  0.7 7.0 %collective-permute-start = (bf16[1,8,1024]{2,1,0:T(8,128)(2,1)S(1)}, bf16[1,8,1024]{2,1,0:T(8,128)(2,1)S(1)}, u32[]{:S(2)}, u32[]{:S(2)}) collective-permute-start(bf16[1,8,1024]{2,1,0:T(8,128)(2,1)S(1)} %slice.3), channel_id=1, source_target_pairs={{0,1},{1,2},{2,3},{3,4},{4,5},{5,6},{6,7},{7,8},{8,9},{9,10},{10,1... | collective-permute-start | bytes 49160 | tf_op jit(solution)/shard_map/ppermute | solution.py:433
  5.4 0.7 %copy-start.2 = (s32[1,8]{1,0:T(1,128)S(1)}, s32[1,8]{1,0:T(1,128)}, u32[]{:S(2)}) copy-start(s32[1,8]{1,0:T(1,128)} %flag_ref.1) | copy-start | bytes 100
  7.6 14.5 %collective-permute-start.2 = (bf16[400,1024]{1,0:T(8,128)(2,1)S(1)}, bf16[400,1024]{1,0:T(8,128)(2,1)S(1)}, u32[]{:S(2)}, u32[]{:S(2)}) collective-permute-start(bf16[400,1024]{1,0:T(8,128)(2,1)S(1)} %get-tuple-element.18.early_ref.refs_1_.refs_2_.refs_0_), channel_id=1, source_target_pairs={{1,0},{2,1},{3,2},{4,3},{5,4},{6,5},{7,6},{8,7},{9,8},{10,9},{11,1... | collective-permute-start | bytes 2457608 | tf_op jit(solution)/shard_map/ppermute | solution.py:433
  7.7 16.6 %collective-permute-start.4 = (bf16[128,1024]{1,0:T(8,128)(2,1)S(1)}, bf16[128,1024]{1,0:T(8,128)(2,1)S(1)}, u32[]{:S(2)}, u32[]{:S(2)}) collective-permute-start(bf16[128,1024]{1,0:T(8,128)(2,1)S(1)} %get-tuple-element.26.late_ref), channel_id=1, source_target_pairs={{1,0},{2,1},{3,2},{4,3},{5,4},{6,5},{7,6},{8,7},{9,8},{10,9},{11,1... | collective-permute-start | bytes 786440 | tf_op jit(solution)/shard_map/ppermute | solution.py:433
  17.5 16.6 %collective-permute-start.1 = (bf16[528,1024]{1,0:T(8,128)(2,1)S(1)}, bf16[528,1024]{1,0:T(8,128)(2,1)S(1)}, u32[]{:S(2)}, u32[]{:S(2)}) collective-permute-start(bf16[528,1024]{1,0:T(8,128)(2,1)S(1)} %get-tuple-element.22), channel_id=1, source_target_pairs={{3,1},{5,3},{7,5},{9,7},{11,9},{13,11},{15,13},{1,15},{19,17},{21,... | collective-permute-start | bytes 3244040 | tf_op jit(solution)/shard_map/ppermute | solution.py:433
  22.1 3.7 %copy-start.1 = (bf16[1024,512]{1,0:T(8,128)(2,1)S(1)}, bf16[1024,512]{1,0:T(8,128)(2,1)}, u32[]{:S(2)}) copy-start(bf16[1024,512]{1,0:T(8,128)(2,1)} %constant.5.clone.refs_4_) | copy-start | bytes 3145732
  22.1 12.1 %collective-permute-start.3 = (bf16[400,1024]{1,0:T(8,128)(2,1)S(1)}, bf16[400,1024]{1,0:T(8,128)(2,1)S(1)}, u32[]{:S(2)}, u32[]{:S(2)}) collective-permute-start(bf16[400,1024]{1,0:T(8,128)(2,1)S(1)} %collective-permute-done.2.refs_0_.refs_3_.refs_1_.odd_ref), channel_id=1, source_target_pairs={{1,0},{0,1},{3,2},{2,3},{5,4},{4,5},{7,6},{6,7},{9,8},{8,9},{11,10... | collective-permute-start | bytes 2457608 | tf_op jit(solution)/shard_map/ppermute | solution.py:433
  24.3 8.1 %collective-permute-start.5 = (bf16[128,1024]{1,0:T(8,128)(2,1)S(1)}, bf16[128,1024]{1,0:T(8,128)(2,1)S(1)}, u32[]{:S(2)}, u32[]{:S(2)}) collective-permute-start(bf16[128,1024]{1,0:T(8,128)(2,1)S(1)} %collective-permute-done.4.refs_0_), channel_id=1, source_target_pairs={{1,0},{0,1},{3,2},{2,3},{5,4},{4,5},{7,6},{6,7},{9,8},{8,9},{11,10... | collective-permute-start | bytes 786440 | tf_op jit(solution)/shard_map/ppermute | solution.py:433

commit v5 on v4

--- a/solution.py
+++ b/solution.py
@@ -191,7 +191,12 @@
             left_ref[:, pl.ds(at, 2 * F8), :] = jnp.concatenate(both, axis=1).astype(bf16)
         return 0
 
-    lax.fori_loop(0, channels // step, chunk, 0)
+    def two(s, _):
+        chunk(2 * s, 0)
+        chunk(2 * s + 1, 0)
+        return 0
+
+    lax.fori_loop(0, channels // step // 2, two, 0)
 
 
 def left_side(early, late, before, forward, windows):

time: 43.8 us -> 43.5 us (level)
  no operation moved by 1% of the time
where the time goes in v5:
time: 43.5 us; the launch traced here: 43.3 us
  Pallas kernels  27.8 us (64%)
  starting transfers between devices  12.3 us (28%)
  waiting for transfers between devices  1.53 us (4%)
  local copies, waits for them, and re-layouts  1.38 us (3%)
    pallas_call x2, Pallas kernels, correlate(): pl.pallas_call(kernel, in_specs=in_specs, out_specs=pl.BlockSpec(memory_s...  13.2 us
    ppermute x6, starting transfers between devices, permute(): return lax.ppermute(x, 'blk', route)  12.3 us
    pallas_call x1, Pallas kernels, left_side(): pl.pallas_call(functools.partial(left_kernel, step=16, windows=windows),...  7.36 us
    pallas_call x3, Pallas kernels, right_side(): pl.pallas_call(kernel, in_specs=[VMEM_SPEC] * len(operands), out_specs=VM...  5.64 us
    pallas_call x1, Pallas kernels, travelling(): pl.pallas_call(functools.partial(block_kernel, step=step), in_specs=[pl.B...  1.56 us
    ppermute x6, waiting for transfers between devices, permute(): return lax.ppermute(x, 'blk', route)  1.53 us
  transfers between devices with their start and end apart: 6, of which 1 were waited for; matrix products, arithmetic and copies ran while one was open for 0% of the time, Pallas kernels for 43%

profile of v5, /device:TPU:1, one launch (start us, length us, event | category | flops | bytes accessed | tf_op | source)
XLA Modules:
  0.0 43.3 jit_solution(1685811702810150616)
XLA Ops:
  0.0 0.7 %slice.3 = bf16[1,8,1024]{2,1,0:T(8,128)(2,1)S(1)} slice(bf16[64,8,1024]{2,1,0:T(8,128)(2,1)} %trace_ref), slice={[63:64], [0:8], [0:1024]} | slice | bytes 32768 | tf_op jit(solution)/shard_map/slice | solution.py:441
  0.7 4.7 %collective-permute-start = (bf16[1,8,1024]{2,1,0:T(8,128)(2,1)S(1)}, bf16[1,8,1024]{2,1,0:T(8,128)(2,1)S(1)}, u32[]{:S(2)}, u32[]{:S(2)}) collective-permute-start(bf16[1,8,1024]{2,1,0:T(8,128)(2,1)S(1)} %slice.3), channel_id=1, source_target_pairs={{0,1},{1,2},{2,3},{3,4},{4,5},{5,6},{6,7},{7,8},{8,9},{9,10},{10,1... | collective-permute-start | bytes 49160 | tf_op jit(solution)/shard_map/ppermute | solution.py:438
  5.4 0.0 copy-start.2
  5.4 0.6 %copy-done.2 = s32[1,8]{1,0:T(1,128)S(1)} copy-done((s32[1,8]{1,0:T(1,128)S(1)}, s32[1,8]{1,0:T(1,128)}, u32[]{:S(2)}) %copy-start.2) | copy-done | bytes 56
  6.0 1.6 %travelling.1 = (bf16[400,1024]{1,0:T(8,128)(2,1)S(1)}, bf16[128,1024]{1,0:T(8,128)(2,1)S(1)}) custom-call(s32[1,8]{1,0:T(1,128)S(1)} %copy-done.2, bf16[64,8,1024]{2,1,0:T(8,128)(2,1)} %trace_ref), custom_call_target="tpu_custom_call" | custom-call | flops 10000000000 | bytes 2097152 | tf_op jit(solution)/shard_map/travelling/pallas_call | solution.py:108
  7.6 0.1 collective-permute-start.2
  7.7 0.0 collective-permute-done.before_ref
  7.7 2.2 %collective-permute-start.4 = (bf16[128,1024]{1,0:T(8,128)(2,1)S(1)}, bf16[128,1024]{1,0:T(8,128)(2,1)S(1)}, u32[]{:S(2)}, u32[]{:S(2)}) collective-permute-start(bf16[128,1024]{1,0:T(8,128)(2,1)S(1)} %get-tuple-element.26.late_ref), channel_id=1, source_target_pairs={{1,0},{2,1},{3,2},{4,3},{5,4},{6,5},{7,6},{8,7},{9,8},{10,9},{11,1... | collective-permute-start | bytes 786440 | tf_op jit(solution)/shard_map/ppermute | solution.py:438
  9.9 7.4 %left_side.1 = (bf16[64,256,256]{2,1,0:T(8,128)(2,1)S(1)}, bf16[528,1024]{1,0:T(8,128)(2,1)S(1)}) custom-call(bf16[400,1024]{1,0:T(8,128)(2,1)S(1)} %get-tuple-element.18.early_ref.refs_1_.refs_2_.refs_0_, bf16[128,1024]{1,0:T(8,128)(2,1)S(1)} %get-tuple-element.26.late_ref, bf16[1,8,1024]{2,1,0:T(8,128)(2,1)S(1)} %collective-permute-done.before_ref, ...), custom_call_target="tpu_custom_call" | custom-call | flops 99999997952 | bytes 12582912 | tf_op jit(solution)/shard_map/left_side/pallas_call | solution.py:206
  17.3 4.7 %collective-permute-start.1 = (bf16[528,1024]{1,0:T(8,128)(2,1)S(1)}, bf16[528,1024]{1,0:T(8,128)(2,1)S(1)}, u32[]{:S(2)}, u32[]{:S(2)}) collective-permute-start(bf16[528,1024]{1,0:T(8,128)(2,1)S(1)} %get-tuple-element.22), channel_id=1, source_target_pairs={{3,1},{5,3},{7,5},{9,7},{11,9},{13,11},{15,13},{1,15},{19,17},{21,... | collective-permute-start | bytes 3244040 | tf_op jit(solution)/shard_map/ppermute | solution.py:438
  22.0 0.0 collective-permute-done.2.refs_0_.refs_3_.refs_1_.odd_ref
  22.0 0.0 copy-start.1
  22.0 0.1 collective-permute-start.3
  22.1 2.1 %right_side.3.refs_2_ = bf16[3,64,64,256]{3,2,1,0:T(8,128)(2,1)S(1)} custom-call(bf16[400,1024]{1,0:T(8,128)(2,1)S(1)} %collective-permute-done.2.refs_0_.refs_3_.refs_1_.odd_ref, bf16[400,1024]{1,0:T(8,128)(2,1)S(1)} %get-tuple-element.18.early_ref.refs_1_.refs_2_.refs_0_, bf16[1024,1024]{1,0:T(8,128)(2,1)S(1)} %copy-done), custom_call_target="tpu_custom_call" | custom-call | flops 2000000000 | bytes 5242880 | tf_op jit(solution)/shard_map/right_side/pallas_call | solution.py:311
  24.2 0.0 collective-permute-done.4.refs_0_
  24.3 0.6 %collective-permute-start.5 = (bf16[128,1024]{1,0:T(8,128)(2,1)S(1)}, bf16[128,1024]{1,0:T(8,128)(2,1)S(1)}, u32[]{:S(2)}, u32[]{:S(2)}) collective-permute-start(bf16[128,1024]{1,0:T(8,128)(2,1)S(1)} %collective-permute-done.4.refs_0_), channel_id=1, source_target_pairs={{1,0},{0,1},{3,2},{2,3},{5,4},{4,5},{7,6},{6,7},{9,8},{8,9},{11,10... | collective-permute-start | bytes 786440 | tf_op jit(solution)/shard_map/ppermute | solution.py:438
  24.8 0.9 %right_side.5.refs_3_ = bf16[1,64,64,256]{3,2,1,0:T(8,128)(2,1)S(1)} custom-call(bf16[128,1024]{1,0:T(8,128)(2,1)S(1)} %collective-permute-done.4.refs_0_, bf16[400,1024]{1,0:T(8,128)(2,1)S(1)} %collective-permute-done.2.refs_0_.refs_3_.refs_1_.odd_ref, bf16[400,1024]{1,0:T(8,128)(2,1)S(1)} %get-tuple-element.18.early_ref.refs_1_.refs_2_.refs_0_, ...), custom_call_target="tpu_custom_call" | custom-call | flops 2000000000 | bytes 5242880 | tf_op jit(solution)/shard_map/right_side/pallas_call | solution.py:311
  25.8 0.0 copy-done.1
  25.8 6.6 %correlate.2.refs_5_ = bf16[2,1,64,64,512]{4,3,2,1,0:T(8,128)(2,1)} custom-call(bf16[400,1024]{1,0:T(8,128)(2,1)S(1)} %collective-permute-done.2.refs_0_.refs_3_.refs_1_.odd_ref, bf16[400,1024]{1,0:T(8,128)(2,1)S(1)} %get-tuple-element.18.early_ref.refs_1_.refs_2_.refs_0_, bf16[64,256,256]{2,1,0:T(8,128)(2,1)S(1)} %get-tuple-element.25.refs_1_.refs_2_, ...), custom_call_target="tpu_custom_call" | custom-call | flops 7000000000 | bytes 20971520 | tf_op jit(solution)/shard_map/correlate/pallas_call | solution.py:414
  32.4 0.0 collective-permute-done.5.refs_2_
  32.4 1.5 %collective-permute-done.1.refs_0_.odd_ref = bf16[528,1024]{1,0:T(8,128)(2,1)S(1)} collective-permute-done((bf16[528,1024]{1,0:T(8,128)(2,1)S(1)}, bf16[528,1024]{1,0:T(8,128)(2,1)S(1)}, u32[]{:S(2)}, u32[]{:S(2)}) %collective-permute-start.1) | collective-permute-done | bytes 1081376 | tf_op jit(solution)/shard_map/ppermute | solution.py:438
  33.9 0.0 collective-permute-done.3.refs_1_.refs_0_
  33.9 2.6 %right_side.4.refs_3_ = bf16[4,64,64,256]{3,2,1,0:T(8,128)(2,1)S(1)} custom-call(bf16[528,1024]{1,0:T(8,128)(2,1)S(1)} %collective-permute-done.1.refs_0_.odd_ref, bf16[400,1024]{1,0:T(8,128)(2,1)S(1)} %collective-permute-done.3.refs_1_.refs_0_, bf16[128,1024]{1,0:T(8,128)(2,1)S(1)} %collective-permute-done.5.refs_2_, ...), custom_call_target="tpu_custom_call" | custom-call | flops 2000000000 | bytes 5242880 | tf_op jit(solution)/shard_map/right_side/pallas_call | solution.py:311
  36.5 6.6 %correlate.3 = bf16[2,1,64,64,512]{4,3,2,1,0:T(8,128)(2,1)} custom-call(bf16[528,1024]{1,0:T(8,128)(2,1)S(1)} %collective-permute-done.1.refs_0_.odd_ref, bf16[400,1024]{1,0:T(8,128)(2,1)S(1)} %collective-permute-done.3.refs_1_.refs_0_, bf16[400,1024]{1,0:T(8,128)(2,1)S(1)} %get-tuple-element.18.early_ref.refs_1_.refs_2_.refs_0_, ...), custom_call_target="tpu_custom_call", output_to_operand_aliasing={{}: (6, {})} | custom-call | flops 7000000000 | bytes 20971520 | tf_op jit(solution)/shard_map/correlate/pallas_call | solution.py:414
  (2 shorter events, 0.0 us)
Async XLA Ops:
  0.7 9.2 %copy-start = (bf16[1024,1024]{1,0:T(8,128)(2,1)S(1)}, bf16[1024,1024]{1,0:T(8,128)(2,1)}, u32[]{:S(2)}) copy-start(bf16[1024,1024]{1,0:T(8,128)(2,1)} %constant.4.clone.forward_ref.refs_2_.refs_4_.refs_3_) | copy-start | bytes 6291460
  0.7 7.0 %collective-permute-start = (bf16[1,8,1024]{2,1,0:T(8,128)(2,1)S(1)}, bf16[1,8,1024]{2,1,0:T(8,128)(2,1)S(1)}, u32[]{:S(2)}, u32[]{:S(2)}) collective-permute-start(bf16[1,8,1024]{2,1,0:T(8,128)(2,1)S(1)} %slice.3), channel_id=1, source_target_pairs={{0,1},{1,2},{2,3},{3,4},{4,5},{5,6},{6,7},{7,8},{8,9},{9,10},{10,1... | collective-permute-start | bytes 49160 | tf_op jit(solution)/shard_map/ppermute | solution.py:438
  5.4 0.7 %copy-start.2 = (s32[1,8]{1,0:T(1,128)S(1)}, s32[1,8]{1,0:T(1,128)}, u32[]{:S(2)}) copy-start(s32[1,8]{1,0:T(1,128)} %flag_ref.1) | copy-start | bytes 100
  7.6 14.4 %collective-permute-start.2 = (bf16[400,1024]{1,0:T(8,128)(2,1)S(1)}, bf16[400,1024]{1,0:T(8,128)(2,1)S(1)}, u32[]{:S(2)}, u32[]{:S(2)}) collective-permute-start(bf16[400,1024]{1,0:T(8,128)(2,1)S(1)} %get-tuple-element.18.early_ref.refs_1_.refs_2_.refs_0_), channel_id=1, source_target_pairs={{1,0},{2,1},{3,2},{4,3},{5,4},{6,5},{7,6},{8,7},{9,8},{10,9},{11,1... | collective-permute-start | bytes 2457608 | tf_op jit(solution)/shard_map/ppermute | solution.py:438
  7.7 16.6 %collective-permute-start.4 = (bf16[128,1024]{1,0:T(8,128)(2,1)S(1)}, bf16[128,1024]{1,0:T(8,128)(2,1)S(1)}, u32[]{:S(2)}, u32[]{:S(2)}) collective-permute-start(bf16[128,1024]{1,0:T(8,128)(2,1)S(1)} %get-tuple-element.26.late_ref), channel_id=1, source_target_pairs={{1,0},{2,1},{3,2},{4,3},{5,4},{6,5},{7,6},{8,7},{9,8},{10,9},{11,1... | collective-permute-start | bytes 786440 | tf_op jit(solution)/shard_map/ppermute | solution.py:438
  17.3 16.6 %collective-permute-start.1 = (bf16[528,1024]{1,0:T(8,128)(2,1)S(1)}, bf16[528,1024]{1,0:T(8,128)(2,1)S(1)}, u32[]{:S(2)}, u32[]{:S(2)}) collective-permute-start(bf16[528,1024]{1,0:T(8,128)(2,1)S(1)} %get-tuple-element.22), channel_id=1, source_target_pairs={{3,1},{5,3},{7,5},{9,7},{11,9},{13,11},{15,13},{1,15},{19,17},{21,... | collective-permute-start | bytes 3244040 | tf_op jit(solution)/shard_map/ppermute | solution.py:438
  22.0 3.7 %copy-start.1 = (bf16[1024,512]{1,0:T(8,128)(2,1)S(1)}, bf16[1024,512]{1,0:T(8,128)(2,1)}, u32[]{:S(2)}) copy-start(bf16[1024,512]{1,0:T(8,128)(2,1)} %constant.5.clone.refs_4_) | copy-start | bytes 3145732
  22.0 11.9 %collective-permute-start.3 = (bf16[400,1024]{1,0:T(8,128)(2,1)S(1)}, bf16[400,1024]{1,0:T(8,128)(2,1)S(1)}, u32[]{:S(2)}, u32[]{:S(2)}) collective-permute-start(bf16[400,1024]{1,0:T(8,128)(2,1)S(1)} %collective-permute-done.2.refs_0_.refs_3_.refs_1_.odd_ref), channel_id=1, source_target_pairs={{1,0},{0,1},{3,2},{2,3},{5,4},{4,5},{7,6},{6,7},{9,8},{8,9},{11,10... | collective-permute-start | bytes 2457608 | tf_op jit(solution)/shard_map/ppermute | solution.py:438
  24.3 8.1 %collective-permute-start.5 = (bf16[128,1024]{1,0:T(8,128)(2,1)S(1)}, bf16[128,1024]{1,0:T(8,128)(2,1)S(1)}, u32[]{:S(2)}, u32[]{:S(2)}) collective-permute-start(bf16[128,1024]{1,0:T(8,128)(2,1)S(1)} %collective-permute-done.4.refs_0_), channel_id=1, source_target_pairs={{1,0},{0,1},{3,2},{2,3},{5,4},{4,5},{7,6},{6,7},{9,8},{8,9},{11,10... | collective-permute-start | bytes 786440 | tf_op jit(solution)/shard_map/ppermute | solution.py:438
